TPU v7x, 256 devices: a whole 4x4x8 slice. The times are simulated.
256 devices in a mesh: ctx: 64 (over x, z, core), mp: 4 (over y).
Axes of the slice: x: 4, y: 4, z: 8, core: 2. Of those that a mesh axis runs over, the one named last changes fastest.
Arguments:
- hidden: bfloat16 [131072, 512], P('ctx', 'mp'), may hold values from -6 to 6
- w_x: bfloat16 [512, 1024], P(None, 'mp'), may hold values from -0.25 to 0.25
- w_z: bfloat16 [512, 1024], P(None, 'mp'), may hold values from -0.25 to 0.25
- w_bc: bfloat16 [512, 256], replicated, may hold values from -0.25 to 0.25
- w_dt: bfloat16 [512, 16], P(None, 'mp'), may hold values from -0.25 to 0.25
- conv_x: float32 [4, 1024], P(None, 'mp'), may hold values from -3 to 3
- conv_bc: float32 [4, 256], replicated, may hold values from -3 to 3
- dt_bias: float32 [16], P('mp'), may hold values from -5 to -3
- decay_rate: float32 [16], P('mp'), may hold values from 2e-06 to 2
- skip_gain: float32 [16], P('mp'), may hold values from 0.1 to 1.9
- norm_gain: float32 [1024], P('mp'), may hold values from 0.1 to 1.9
- w_out: bfloat16 [1024, 512], P('mp'), may hold values from -0.1875 to 0.1875
- piece_lengths: int32 [16], replicated, may hold values from 1 to 65536, 131072 in all
Outputs:
- layer_out: bfloat16 [131072, 512], P('ctx', 'mp')
Inputs may be any that keep to these rules, and one draw needn't show every extreme that they name: `piece_lengths`: the piece lengths add up to 131072, and the longest is exactly 65536.
All inputs are finite; a program needn't handle non-finite values.
Results may differ from a plain program's by a relative error of at most 0.015.
Values may be sent and summed in bfloat16 or wider, within the bound.
No kernel may reach another device: no remote copies, remote signals or barrier semaphores. Data moves between devices by JAX's collectives and lax.ppermute only.
A program may use at most 128 MiB of HBM per device.

v0:
```python
import functools

import jax
import jax.numpy as jnp
import numpy as np
from jax import lax
from jax.experimental import pallas as pl
from jax.experimental.pallas import tpu as pltpu
from jax.sharding import PartitionSpec as P

E = 1024
HEAD_DIM = 64
NSTATE = 128
BLOCK = 256
HEADS_HERE = 4
INNER = HEADS_HERE * HEAD_DIM
PIECES = 16
EPSILON = 1e-05
FAR = -1e30
EDGE = 16
MIX = INNER + NSTATE
QUARTER = NSTATE // 4
RUN = (4, 2)
HERE = 4
BLOCKS = 2 * HERE
PAY = 2 * QUARTER + 16

bf16 = jnp.bfloat16
f32 = jnp.float32


def head_spread():
    out = np.zeros((16, 2 * INNER), np.float32)
    for part in range(2):
        for stream in range(2):
            for h in range(HEADS_HERE):
                first = stream * INNER + h * HEAD_DIM
                out[part * 8 + stream * 4 + h, first : first + HEAD_DIM] = 1.0
    return out


def whole(shape):
    return pl.BlockSpec(shape, lambda *_: (0,) * len(shape))


SMEM = pl.BlockSpec(memory_space=pltpu.SMEM)


def params(mib):
    return pltpu.CompilerParams(
        dimension_semantics=("arbitrary",), vmem_limit_bytes=mib * 1024 * 1024
    )


def cost(flops, nbytes):
    return pl.CostEstimate(flops=int(flops), bytes_accessed=int(nbytes), transcendentals=0)


def bounds_of(pieces_ref):
    total = pieces_ref[0]
    ends = [total]
    for k in range(1, PIECES):
        total = total + pieces_ref[k]
        ends.append(total)
    return ends


def seg_rows(ends, first):
    shape = (8, BLOCK)
    pos = (
        first - 3 + lax.broadcasted_iota(jnp.int32, shape, 0)
        + lax.broadcasted_iota(jnp.int32, shape, 1)
    )
    seg = jnp.zeros(shape, jnp.int32)
    for end in ends:
        seg = seg + (pos >= end).astype(jnp.int32)
    return seg.astype(f32)


def has_boundary(ends, first):
    found = jnp.int32(0)
    for end in ends:
        found = found + ((end > first - 3) & (end <= first + BLOCK + 2)).astype(jnp.int32)
    return found > 0


def split2(rows):
    high = rows.astype(bf16)
    return jnp.concatenate([high, (rows - high.astype(f32)).astype(bf16)], axis=0)


def rows_to_cols(rows, spread):
    return lax.dot_general(
        split2(rows), spread, (((0,), (0,)), ((), ())), preferred_element_type=f32
    )


def row_of(chunk, g):
    return EDGE + g * BLOCK + (g // RUN[chunk]) * 2 * EDGE


def block_of(chunk, g):
    return g + 2 if chunk == 0 else g + 4 * (g // 2)


def load_window(hs, chunk, g):
    at = pl.multiple_of(row_of(chunk, g) - EDGE, EDGE)
    return jnp.concatenate([h[pl.ds(at, BLOCK + 2 * EDGE), :] for h in hs], axis=1)


def silu(v):
    half = 0.5 * v
    return half + half * jnp.tanh(half)


def tap_rows(conv_x, conv_bc):
    return [conv_x[:, 0:128], conv_x[:, 128:256], conv_bc[:, 0:128], conv_bc[:, 128:256]]


def conv_tile(scratch, tile, taps, reverse, masks):
    total = None
    for back in range(4):
        first = back if reverse else EDGE - back
        term = scratch[tile, pl.ds(first, BLOCK), :] * taps[3 - back : 4 - back, :]
        if masks is not None and back:
            row = 3 + back if reverse else 3 - back
            term = term * masks[:, row : row + 1]
        total = term if total is None else total + term
    return silu(total).astype(bf16)


def keep_rounded(scratch, proj):
    for tile in range(scratch.shape[0]):
        scratch[tile] = proj[:, tile * 128 : (tile + 1) * 128].astype(bf16).astype(f32)


def per_head(scalars, shape, axis, width):
    head = lax.broadcasted_iota(jnp.int32, shape, axis) // width % HEADS_HERE
    out = jnp.full(shape, scalars[0], f32)
    for h in range(1, HEADS_HERE):
        out = jnp.where(head == h, scalars[h], out)
    return out


def split_rows(decays):
    at = lax.broadcasted_iota(jnp.int32, (16, INNER), 0)
    out = jnp.zeros((16, INNER), f32)
    for k, decay in enumerate(decays):
        high = decay.astype(bf16).astype(f32)
        out = jnp.where(at == 2 * k, high, jnp.where(at == 2 * k + 1, decay - high, out))
    return out.astype(bf16)


def decays_of(rows):
    wide = rows.astype(f32)
    return [wide[2 * k : 2 * k + 1, :] + wide[2 * k + 1 : 2 * k + 2, :] for k in range(2)]


def row_quantities(
    chunk, ends, origin, hs, wdt, dt_bias, rate, spread, cum_o, dt_o, fs_o, same_s, te_s, blockdec
):
    raw = []
    for b in range(HERE):
        at = row_of(chunk, b)
        block = jnp.concatenate([h[at : at + BLOCK, :] for h in hs], axis=1)
        raw.append(
            lax.dot_general(wdt[...], block, (((1,), (1,)), ((), ())), preferred_element_type=f32)
        )
    shape = (8 * HERE, BLOCK)
    v = jnp.concatenate(raw, axis=0).astype(bf16).astype(f32) + per_head(dt_bias, shape, 0, 1)
    dt = jnp.maximum(v, 0.0) + jnp.log1p(jnp.exp(-jnp.abs(v)))
    logd = -dt * per_head(rate, shape, 0, 1)
    high = logd.astype(bf16)
    rest = logd - high.astype(f32)
    middle = rest.astype(bf16)
    low = (rest - middle.astype(f32)).astype(bf16)
    row_at = lax.broadcasted_iota(jnp.int32, (BLOCK, BLOCK), 0)
    col_at = lax.broadcasted_iota(jnp.int32, (BLOCK, BLOCK), 1)
    summed = []
    for keep in (row_at <= col_at, row_at >= col_at):
        ones = keep.astype(f32).astype(bf16)
        summed.append(sum(jnp.dot(p, ones, preferred_element_type=f32) for p in (low, middle, high)))
    forward = lax.broadcasted_iota(jnp.int32, (8, BLOCK), 0) < HEADS_HERE
    spread_f = spread[0:8, :].astype(f32)
    for b in range(HERE):
        rows = slice(b * 8, (b + 1) * 8)
        cols = slice(b * BLOCK, (b + 1) * BLOCK)
        cum = jnp.where(forward, summed[0][rows], summed[1][rows])
        dt_b = dt[rows]
        seg = seg_rows(ends, origin + block_of(chunk, b) * BLOCK)
        same_s[b] = (seg == seg[3:4, :]).astype(f32)
        own = jnp.broadcast_to(seg[3:4, :], (8, BLOCK))
        seg_end = jnp.where(forward, seg[3:4, BLOCK - 1 : BLOCK], seg[3:4, 0:1])
        seg_in = jnp.where(forward, seg[2:3, 0:1], seg[4:5, BLOCK - 1 : BLOCK])
        total = jnp.where(forward, cum[:, BLOCK - 1 : BLOCK], cum[:, 0:1])
        to_end = jnp.exp(total - cum) * (own == seg_end).astype(f32) * dt_b
        block_decay = jnp.exp(total) * (seg_end == seg_in).astype(f32)
        cum_o[:, cols] = cum
        dt_o[:, cols] = dt_b
        fs_o[:, cols] = jnp.exp(cum) * (own == seg_in).astype(f32)
        te_s[b] = split2(to_end)
        decay_row = jnp.sum(
            jnp.concatenate([block_decay, block_decay], axis=1) * spread_f, axis=0, keepdims=True
        )
        blockdec[b] = jnp.broadcast_to(decay_row, (8, 2 * INNER))


def k1_body(chunk, pieces, meta, dt_bias, rate, h0, h1, h2, h3, w_f, w_r, wdt, conv_x, conv_bc, spread, *rest):
    if chunk == 0:
        xb_f, xb_r, cum_o, dt_o, fs_o, added, blockdec, sf, sr, same_s, te_s = rest
    else:
        added_0, blockdec_0, *rest = rest
        xb_f, xb_r, cum_o, dt_o, fs_o, start_o, decay_o, p0, p1, p2, p3 = rest[:11]
        sf, sr, same_s, te_s, added, blockdec, total_s = rest[11:]
    g = pl.program_id(0)
    ends = bounds_of(pieces)
    first = meta[0] + block_of(chunk, g) * BLOCK
    hs = (h0, h1, h2, h3)

    @pl.when(g == 0)
    def _():
        row_quantities(
            chunk, ends, meta[0], hs, wdt, dt_bias, rate, spread, cum_o, dt_o, fs_o, same_s, te_s, blockdec
        )

    crosses = has_boundary(ends, first)

    def states(masked):
        window = load_window(hs, chunk, g)
        masks = same_s[g].T if masked else None
        taps = tap_rows(conv_x, conv_bc)
        wide = lax.dot_general(
            te_s[g], spread[...], (((0,), (0,)), ((), ())), preferred_element_type=f32
        )
        keep_rounded(sf, jnp.dot(window[: EDGE + BLOCK], w_f[...], preferred_element_type=f32))
        keep_rounded(sr, jnp.dot(window[EDGE:], w_r[...], preferred_element_type=f32))
        for stream, scratch, ref in ((0, sf, xb_f), (1, sr, xb_r)):
            scaled = []
            for tile in (0, 1):
                x = conv_tile(scratch, tile, taps[tile], stream == 1, masks)
                ref[:, tile * 128 : (tile + 1) * 128] = x
                at = stream * INNER + tile * 128
                scaled.append((x.astype(f32) * wide[:, at : at + 128]).astype(bf16))
            b = conv_tile(scratch, 2, taps[2], stream == 1, masks)
            ref[:, INNER:MIX] = b
            added[stream, g] = lax.dot_general(
                b, jnp.concatenate(scaled, axis=1), (((0,), (0,)), ((), ())), preferred_element_type=f32
            )

    pl.when(crosses)(lambda: states(True))
    pl.when(jnp.logical_not(crosses))(lambda: states(False))
    if chunk == 0:
        return

    @pl.when(g == HERE - 1)
    def _():
        sources = {block_of(0, k): (added_0, blockdec_0, k) for k in range(HERE)}
        sources.update({block_of(1, k): (added, blockdec, k) for k in range(HERE)})
        decays = []
        for stream in range(2):
            state = jnp.zeros((NSTATE, INNER), f32)
            decay = jnp.ones((1, INNER), f32)
            for step in range(BLOCKS):
                b = step if stream == 0 else BLOCKS - 1 - step
                start_o[stream, b] = state
                decay_o[stream, b] = jnp.broadcast_to(decay, (8, INNER))
                states_ref, decays_ref, k = sources[b]
                d = decays_ref[k, 0:1, stream * INNER : (stream + 1) * INNER]
                state = d * state + states_ref[stream, k]
                decay = decay * d
            total_s[stream] = state
            decays.append(decay)
        rows = split_rows(decays)
        for s, ref in enumerate((p0, p1, p2, p3)):
            at = pl.multiple_of(lax.rem(meta[1] + s, 4) * QUARTER, QUARTER)
            ref[0:QUARTER, :] = total_s[0, pl.ds(at, QUARTER), :].astype(bf16)
            ref[QUARTER : 2 * QUARTER, :] = total_s[1, pl.ds(at, QUARTER), :].astype(bf16)
            ref[2 * QUARTER : PAY, :] = rows


def local_states(chunk, pieces, meta, dt_bias, rate, hs, w_f, w_r, wdt, conv_x, conv_bc, spread, others=()):
    rows = HERE * BLOCK
    row = pl.BlockSpec((BLOCK, MIX), lambda g: (g, 0))
    fixed = [*hs, w_f, w_r, wdt, conv_x, conv_bc, spread, *others]
    added = jax.ShapeDtypeStruct((2, HERE, NSTATE, INNER), f32)
    blockdec = jax.ShapeDtypeStruct((HERE, 8, 2 * INNER), f32)
    shapes = [
        jax.ShapeDtypeStruct((rows, MIX), bf16),
        jax.ShapeDtypeStruct((rows, MIX), bf16),
        jax.ShapeDtypeStruct((8, rows), f32),
        jax.ShapeDtypeStruct((8, rows), f32),
        jax.ShapeDtypeStruct((8, rows), f32),
    ]
    scratch = [
        pltpu.VMEM((MIX // 128, EDGE + BLOCK, 128), f32),
        pltpu.VMEM((MIX // 128, EDGE + BLOCK, 128), f32),
        pltpu.VMEM((HERE, 8, BLOCK), f32),
        pltpu.VMEM((HERE, 16, BLOCK), bf16),
    ]
    if chunk == 0:
        shapes += [added, blockdec]
    else:
        shapes += [
            jax.ShapeDtypeStruct((2, BLOCKS, NSTATE, INNER), f32),
            jax.ShapeDtypeStruct((2, BLOCKS, 8, INNER), f32),
        ] + [jax.ShapeDtypeStruct((PAY, INNER), bf16)] * 4
        scratch += [pltpu.VMEM(a.shape, f32) for a in (added, blockdec)]
        scratch += [pltpu.VMEM((2, NSTATE, INNER), f32)]
    return pl.pallas_call(
        functools.partial(k1_body, chunk),
        grid=(HERE,),
        in_specs=[SMEM] * 4 + [whole(a.shape) for a in fixed],
        out_specs=[row, row] + [whole(s.shape) for s in shapes[2:]],
        out_shape=shapes,
        scratch_shapes=scratch,
        compiler_params=params(24),
        cost_estimate=cost(rows * 6e6, rows * 4000),
        name="local_states",
    )(pieces, meta, dt_bias, rate, *fixed)


def k2_body(
    chunk, base, n_alias, pieces, meta, skip_gain, h0, h1, h2, h3, w_f, w_r, conv_x, conv_bc,
    xb_f, xb_r, cum_i, dt_i, *rest,
):
    c_f, c_r, y_f, y_r, z_f, z_r, sf, sr, open_mask = rest[n_alias:]
    step = pl.program_id(0)
    g = step + base
    ends = bounds_of(pieces)
    first = meta[0] + block_of(chunk, g) * BLOCK
    row_at = lax.broadcasted_iota(jnp.int32, (BLOCK, BLOCK), 0)
    col_at = lax.broadcasted_iota(jnp.int32, (BLOCK, BLOCK), 1)
    half = BLOCK // 2

    @pl.when(step == 0)
    def _():
        open_mask[0] = jnp.where(row_at >= col_at, 0.0, FAR)
        open_mask[1] = jnp.where(row_at <= col_at, 0.0, FAR)

    crosses = has_boundary(ends, first)

    @pl.when(crosses)
    def _():
        seg = seg_rows(ends, first)
        together = seg.T[:, 3:4] == seg[3:4, :]
        open_mask[2] = jnp.where(together & (row_at >= col_at), 0.0, FAR)
        open_mask[3] = jnp.where(together & (row_at <= col_at), 0.0, FAR)

    def mix(masked):
        window = load_window((h0, h1, h2, h3), chunk, g)
        masks = None
        if masked:
            seg = seg_rows(ends, first)
            masks = (seg == seg[3:4, :]).astype(f32).T
        proj_f = jnp.dot(window[: EDGE + BLOCK], w_f[...], preferred_element_type=f32)
        proj_r = jnp.dot(window[EDGE:], w_r[...], preferred_element_type=f32)
        keep_rounded(sf, proj_f)
        keep_rounded(sr, proj_r)
        z_f[...] = silu(proj_f[EDGE:, NSTATE:].astype(bf16).astype(f32))
        z_r[...] = silu(proj_r[0:BLOCK, NSTATE:].astype(bf16).astype(f32))
        taps = tap_rows(conv_x, conv_bc)[3]
        cum = cum_i[...]
        cum_t = cum.T
        log_dt = jnp.log(dt_i[...]) - cum
        lane_head = lax.broadcasted_iota(jnp.int32, (BLOCK, INNER), 1) // HEAD_DIM
        skip = per_head(skip_gain, (1, INNER), 1, HEAD_DIM)
        for stream, xb, scratch, c_ref, y_ref in ((0, xb_f, sf, c_f, y_f), (1, xb_r, sr, c_r, y_r)):
            c_rows = conv_tile(scratch, 0, taps, stream == 1, masks)
            c_ref[...] = c_rows
            x = xb[:, 0:INNER]
            b = xb[:, INNER:MIX]
            heads = [jnp.where(lane_head == h, x, jnp.zeros_like(x)) for h in range(HEADS_HERE)]
            for part in range(2):
                rows = slice(part * half, (part + 1) * half)
                if stream == 0:
                    cols = slice(0, half) if part == 0 else slice(0, BLOCK)
                else:
                    cols = slice(0, BLOCK) if part == 0 else slice(half, BLOCK)
                scores = lax.dot_general(
                    c_rows[rows, :], b[cols, :], (((1,), (1,)), ((), ())), preferred_element_type=f32
                )
                mask = open_mask[(2 if masked else 0) + stream, rows, cols]
                total = x[rows, :].astype(f32) * skip
                for h in range(HEADS_HERE):
                    at = stream * HEADS_HERE + h
                    gap = (cum_t[rows, at : at + 1] + log_dt[at : at + 1, cols]) + mask
                    weight = (jnp.exp(gap) * scores).astype(bf16)
                    total = total + jnp.dot(weight, heads[h][cols, :], preferred_element_type=f32)
                y_ref[rows, :] = total

    pl.when(crosses)(lambda: mix(True))
    pl.when(jnp.logical_not(crosses))(lambda: mix(False))


def intra(chunk, part, n_parts, pieces, meta, skip_gain, hs, w_f, w_r, conv_x, conv_bc, xb_f, xb_r, cum, dt, before):
    rows = HERE * BLOCK
    here = HERE // n_parts
    base = part * here
    col = pl.BlockSpec((8, BLOCK), lambda g: (0, g + base))
    mixed = pl.BlockSpec((BLOCK, MIX), lambda g: (g + base, 0))
    c_out = pl.BlockSpec((BLOCK, NSTATE), lambda g: (g + base, 0))
    y_out = pl.BlockSpec((BLOCK, INNER), lambda g: (g + base, 0))
    fixed = [*hs, w_f, w_r, conv_x, conv_bc]
    before = list(before)
    n_in = 3 + len(fixed) + 4
    return pl.pallas_call(
        functools.partial(k2_body, chunk, base, len(before)),
        grid=(here,),
        in_specs=[SMEM] * 3 + [whole(a.shape) for a in fixed] + [mixed, mixed, col, col]
        + [pl.BlockSpec(memory_space=pl.ANY)] * len(before),
        out_specs=[c_out, c_out, y_out, y_out, y_out, y_out],
        out_shape=[jax.ShapeDtypeStruct((rows, NSTATE), bf16)] * 2
        + [jax.ShapeDtypeStruct((rows, INNER), f32)] * 4,
        input_output_aliases={n_in + k: k for k in range(len(before))},
        scratch_shapes=[
            pltpu.VMEM((1, EDGE + BLOCK, 128), f32),
            pltpu.VMEM((1, EDGE + BLOCK, 128), f32),
            pltpu.VMEM((4, BLOCK, BLOCK), f32),
        ],
        compiler_params=params(24),
        cost_estimate=cost(here * BLOCK * 5e6, here * BLOCK * 5000),
        name="intra",
    )(pieces, meta, skip_gain, *fixed, xb_f, xb_r, cum, dt, *before)


def state_rows(ref, stream):
    return ref[stream * QUARTER : (stream + 1) * QUARTER, :].astype(f32)


def put_payload(ref, states, decays):
    for stream in range(2):
        ref[stream * QUARTER : (stream + 1) * QUARTER, :] = states[stream].astype(bf16)
    ref[2 * QUARTER : PAY, :] = split_rows(decays)


def group_body(meta, own, r1, r2, r3, pre_s, pre_a, pay, stage):
    me = meta[1]
    for s, ref in enumerate((own, r1, r2, r3)):
        stage[lax.rem(me - s + 4, 4)] = ref[...]
    states, decays = [], []
    for stream in range(2):
        state = jnp.zeros((QUARTER, INNER), f32)
        decay = jnp.ones((1, INNER), f32)
        for step in range(4):
            k = step if stream == 0 else 3 - step
            pre_s[k, stream] = state
            pre_a[k, stream] = jnp.broadcast_to(decay, (8, INNER))
            one = stage[k]
            d = decays_of(one[2 * QUARTER :])[stream]
            state = d * state + one[stream * QUARTER : (stream + 1) * QUARTER].astype(f32)
            decay = decay * d
        states.append(state)
        decays.append(decay)
    put_payload(pay, states, decays)


def before_digit(place, stream, got):
    low_s, low_a = jnp.zeros((QUARTER, INNER), f32), jnp.ones((1, INNER), f32)
    for s in (1, 2, 3):
        there = s <= place
        state, decay = got[s if stream == 0 else 4 - s]
        low_s = jnp.where(there, low_s + low_a * state, low_s)
        low_a = jnp.where(there, low_a * decay, low_a)
    return low_s, low_a


def middle_body(meta, own, r1, r2, r3, low_o, low_ao, pay):
    digit = meta[2]
    states, decays = [], []
    rows = [decays_of(r[2 * QUARTER : PAY, :]) for r in (own, r1, r2, r3)]
    for stream in range(2):
        got = [(state_rows(r, stream), rows[s][stream]) for s, r in enumerate((own, r1, r2, r3))]
        place = digit if stream == 0 else 3 - digit
        low_s, low_a = before_digit(place, stream, got)
        low_o[stream] = low_s
        low_ao[stream] = jnp.broadcast_to(low_a, (8, INNER))
        total_s, total_a = got[0][1] * low_s + got[0][0], got[0][1] * low_a
        for s in (3, 2, 1):
            there = s > place
            state, decay = got[s if stream == 0 else 4 - s]
            total_s = jnp.where(there, decay * total_s + state, total_s)
            total_a = jnp.where(there, decay * total_a, total_a)
        states.append(total_s)
        decays.append(total_a)
    put_payload(pay, states, decays)


def top_body(meta, r1, r2, r3, low_i, low_ai, pre_s, pre_a, *outs):
    digit = meta[3]
    rows = [None] + [decays_of(r[2 * QUARTER : PAY, :]) for r in (r1, r2, r3)]
    for stream in range(2):
        got = [None] + [
            (state_rows(r, stream), rows[s + 1][stream]) for s, r in enumerate((r1, r2, r3))
        ]
        place = digit if stream == 0 else 3 - digit
        top_s, _ = before_digit(place, stream, got)
        group_s = low_ai[stream, 0:1, :] * top_s + low_i[stream]
        for s, ref in enumerate(outs):
            k = lax.rem(meta[1] + s, 4)
            member = pre_a[k, stream][0:1, :] * group_s + pre_s[k, stream]
            ref[stream * QUARTER : (stream + 1) * QUARTER, :] = member.astype(bf16)


def small_call(body, name, meta, arrays, shapes, scratch=()):
    return pl.pallas_call(
        body,
        grid=(1,),
        in_specs=[SMEM] + [whole(a.shape) for a in arrays],
        out_specs=[whole(s.shape) for s in shapes],
        out_shape=shapes,
        scratch_shapes=list(scratch),
        compiler_params=params(6),
        cost_estimate=cost(2e6, 1e6),
        name=name,
    )(meta, *arrays)


PAYLOAD = jax.ShapeDtypeStruct((PAY, INNER), bf16)


def join_group(meta, arrays):
    shapes = [
        jax.ShapeDtypeStruct((4, 2, QUARTER, INNER), f32),
        jax.ShapeDtypeStruct((4, 2, 8, INNER), f32),
        PAYLOAD,
    ]
    return small_call(group_body, "join_group", meta, arrays, shapes, [pltpu.VMEM((4, PAY, INNER), bf16)])


def join_middle(meta, arrays):
    shapes = [
        jax.ShapeDtypeStruct((2, QUARTER, INNER), f32),
        jax.ShapeDtypeStruct((2, 8, INNER), f32),
        PAYLOAD,
    ]
    return small_call(middle_body, "join_middle", meta, arrays, shapes)


def join_top(meta, arrays):
    shapes = [jax.ShapeDtypeStruct((2 * QUARTER, INNER), bf16)] * 4
    return small_call(top_body, "join_top", meta, arrays, shapes)


def k3_body(meta, c_f, c_r, y_f, y_r, z_f, z_r, fs, starts, decays, q0, q1, q2, q3, gain, spread, *rest):
    g_f, g_r, sums, s_in = rest[-4:]

    @pl.when(pl.program_id(0) == 0)
    def _():
        for s, ref in enumerate((q0, q1, q2, q3)):
            at = pl.multiple_of(lax.rem(meta[1] - s + 4, 4) * QUARTER, QUARTER)
            for stream in range(2):
                s_in[stream, pl.ds(at, QUARTER), :] = state_rows(ref, stream)

    wide = rows_to_cols(fs[...], spread[...])
    out = []
    for stream, c_ref, y_ref, z_ref, g_ref in ((0, c_f, y_f, z_f, g_f), (1, c_r, y_r, z_r, g_r)):
        state = starts[stream, 0] + decays[stream, 0, 0:1, :] * s_in[stream]
        carried = jnp.dot(c_ref[...], state.astype(bf16), preferred_element_type=f32)
        mixed = y_ref[...] + carried * wide[:, stream * INNER : (stream + 1) * INNER]
        gated = mixed * z_ref[...]
        square = gated * gated
        out.append(jnp.sum((square[:, 0:128] + square[:, 128:256]).T, axis=0, keepdims=True))
        g_ref[...] = (gated * gain[...]).astype(bf16)
    sums[...] = jnp.concatenate(out, axis=0)


def gate(chunk, meta, locals_, fs, starts, decays, quarters, gain, spread, before):
    base = chunk * HERE
    m = BLOCKS * BLOCK
    c_in = pl.BlockSpec((BLOCK, NSTATE), lambda g: (g, 0))
    y_in = pl.BlockSpec((BLOCK, INNER), lambda g: (g, 0))
    y_out = pl.BlockSpec((BLOCK, INNER), lambda g: (g + base, 0))
    fixed = [*quarters, gain, spread]
    before = list(before)
    n_in = 1 + 6 + 3 + len(fixed)
    return pl.pallas_call(
        k3_body,
        grid=(HERE,),
        in_specs=[SMEM, c_in, c_in, y_in, y_in, y_in, y_in,
                  pl.BlockSpec((8, BLOCK), lambda g: (0, g)),
                  pl.BlockSpec((2, 1, NSTATE, INNER), lambda g: (0, block_of(chunk, g), 0, 0)),
                  pl.BlockSpec((2, 1, 8, INNER), lambda g: (0, block_of(chunk, g), 0, 0))]
        + [whole(a.shape) for a in fixed] + [pl.BlockSpec(memory_space=pl.ANY)] * len(before),
        out_specs=[y_out, y_out, pl.BlockSpec((2, BLOCK), lambda g: (0, g + base))],
        out_shape=[
            jax.ShapeDtypeStruct((m, INNER), bf16),
            jax.ShapeDtypeStruct((m, INNER), bf16),
            jax.ShapeDtypeStruct((2, m), f32),
        ],
        input_output_aliases={n_in + k: k for k in range(len(before))},
        scratch_shapes=[pltpu.VMEM((2, NSTATE, INNER), f32)],
        compiler_params=params(16),
        cost_estimate=cost(m * 3e5, m * 3000),
        name="gate",
    )(meta, *locals_, fs, starts, decays, *fixed, *before)


def k4_body(g_f, g_r, s0, s1, s2, s3, w_f, w_r, spread, o0, o1, o2, o3):
    total = (s0[...] + s1[...]) + (s2[...] + s3[...])
    scale = lax.rsqrt(total / E + EPSILON)
    scale = jnp.concatenate([scale, jnp.zeros((6, BLOCK), f32)], axis=0)
    wide = rows_to_cols(scale, spread[...])
    out_f = jnp.dot(g_f[...], w_f[...], preferred_element_type=f32)
    out_r = jnp.dot(g_r[...], w_r[...], preferred_element_type=f32)
    for s, ref in enumerate((o0, o1, o2, o3)):
        cols = slice(s * 128, (s + 1) * 128)
        part = out_f[:, cols] * wide[:, 0:128] + out_r[:, cols] * wide[:, 128:256]
        ref[...] = part.astype(ref.dtype)


def project_out(g_f, g_r, sums, w_f, w_r, spread):
    m = g_f.shape[0]
    n = m // BLOCK
    g_in = pl.BlockSpec((BLOCK, INNER), lambda g: (g, 0))
    s_in = pl.BlockSpec((2, BLOCK), lambda g: (0, g))
    o = pl.BlockSpec(
        (BLOCK, 128), lambda g: (jnp.where(g < HERE, block_of(0, g), block_of(1, g - HERE)), 0)
    )
    return pl.pallas_call(
        k4_body,
        grid=(n,),
        in_specs=[g_in, g_in] + [s_in] * 4 + [whole(w_f.shape), whole(w_r.shape), whole(spread.shape)],
        out_specs=[o] * 4,
        out_shape=[jax.ShapeDtypeStruct((m, 128), f32)] + [jax.ShapeDtypeStruct((m, 128), bf16)] * 3,
        compiler_params=params(16),
        cost_estimate=cost(m * 1e6, m * 3000),
        name="project_out",
    )(g_f, g_r, *sums, w_f, w_r, spread)


def row_spread():
    out = np.zeros((16, 256), np.float32)
    for part in range(2):
        out[part * 8, 0:128] = 1.0
        out[part * 8 + 1, 128:256] = 1.0
    return out


def around(array, axis, count, shift):
    return lax.ppermute(array, axis, [(i, (i + shift) % count) for i in range(count)])


def digit_perm(count, stride, shift):
    pairs = []
    for i in range(count):
        d = (i // stride) % 4
        pairs.append((i, i + (((d + shift) % 4) - d) * stride))
    return pairs


INTRA_PARTS = 2


def shards(
    hidden, w_x, w_z, w_bc, w_dt, conv_x, conv_bc, dt_bias, decay_rate, skip_gain, norm_gain, w_out,
    piece_lengths,
):
    rows = hidden.shape[0]
    ctx, mp = lax.axis_index("ctx"), lax.axis_index("mp")
    n_ctx, n_mp = lax.axis_size("ctx"), lax.axis_size("mp")

    run = rows // 4
    middle = hidden[run - EDGE : 3 * run + EDGE]
    hs_0 = [middle] + [around(middle, "mp", n_mp, s) for s in range(1, n_mp)]
    low = lax.ppermute(hidden[rows - EDGE :], "ctx", [(i, i + 1) for i in range(n_ctx - 1)])
    high = lax.ppermute(hidden[:EDGE], "ctx", [(i + 1, i) for i in range(n_ctx - 1)])
    outer = jnp.concatenate([low, hidden[: run + EDGE], hidden[3 * run - EDGE :], high], axis=0)
    hs_1 = [outer] + [around(outer, "mp", n_mp, s) for s in range(1, n_mp)]

    width = w_x.shape[0]
    here = width // n_mp
    at = jnp.arange(width, dtype=jnp.int32)
    place = ((mp - at // here) % n_mp) * here + at % here
    pick_f = (place[:, None] == at[None, :]).astype(bf16)
    pick_r = (width - 1 - place[:, None] == at[None, :]).astype(bf16)
    w_1 = jnp.concatenate([w_x, w_bc[:, :NSTATE]], axis=1)
    w_2 = jnp.concatenate([w_bc[:, NSTATE:], w_z], axis=1)
    w_1f, w_1r, w_2f, w_2r = (
        jnp.dot(pick, w, preferred_element_type=f32).astype(bf16)
        for w in (w_1, w_2) for pick in (pick_f, pick_r)
    )
    wdt = jnp.concatenate(
        [jnp.dot(pick, w_dt, preferred_element_type=f32).astype(bf16).T for pick in (pick_f, pick_r)], axis=0
    )
    goal = ((mp + at // here) % n_mp) * here + at % here
    out_pick_f = (goal[None, :] == at[:, None]).astype(bf16)
    out_pick_r = (width - 1 - goal[None, :] == at[:, None]).astype(bf16)
    w_of = jnp.dot(w_out, out_pick_f, preferred_element_type=f32).astype(bf16)
    w_or = jnp.dot(w_out, out_pick_r, preferred_element_type=f32).astype(bf16)

    gain = norm_gain[None, :]
    spread = jnp.asarray(head_spread(), bf16)
    spread_rows = jnp.asarray(row_spread(), bf16)
    meta = jnp.stack([ctx * rows, ctx % 4, (ctx // 4) % 4, (ctx // 16) % 4]).astype(jnp.int32)

    first = (piece_lengths, meta, dt_bias, decay_rate)
    weights_1 = (w_1f, w_1r, wdt, conv_x, conv_bc, spread)
    weights_2 = (w_2f, w_2r, conv_x, conv_bc)

    xb_f, xb_r, cum, dt, fs_0, *middle_states = local_states(0, *first, hs_0, *weights_1)
    locals_0 = intra(
        0, 0, 1, piece_lengths, meta, skip_gain, hs_0, *weights_2, xb_f, xb_r, cum, dt, ()
    )
    hs_1, locals_0 = lax.optimization_barrier((tuple(hs_1), tuple(locals_0)))
    xb_f, xb_r, cum, dt, fs_1, starts, decays, *pays = local_states(
        1, *first, hs_1, *weights_1, middle_states
    )
    locals_1 = ()

    def beside(part, received):
        nonlocal locals_1
        locals_1 = intra(
            1, part, INTRA_PARTS, piece_lengths, meta, skip_gain, hs_1, *weights_2, xb_f, xb_r, cum, dt, locals_1
        )
        received, locals_1 = lax.optimization_barrier((received, tuple(locals_1)))
        return received

    def moved(arrays, stride):
        return [lax.ppermute(a, "ctx", digit_perm(n_ctx, stride, s)) for s, a in zip((1, 2, 3), arrays)]

    pre_s, pre_a, pay = join_group(meta, [pays[0]] + beside(0, moved(pays[1:], 1)))
    low_s, low_a, top = join_middle(meta, [pay] + beside(1, moved([pay] * 3, 4)))
    back = join_top(meta, moved([top] * 3, 16) + [low_s, low_a, pre_s, pre_a])
    quarters = [back[0]] + moved(back[1:], 1)

    gated = gate(0, meta, locals_0, fs_0, starts, decays, quarters, gain, spread, ())
    g_f, g_r, sums = gate(1, meta, locals_1, fs_1, starts, decays, quarters, gain, spread, gated)
    all_sums = [sums] + [around(sums, "mp", n_mp, s) for s in range(1, n_mp)]
    total, *sent = project_out(g_f, g_r, all_sums, w_of, w_or, spread_rows)
    for s, piece in enumerate(sent):
        total = total + around(piece, "mp", n_mp, s + 1).astype(f32)
    return total.astype(bf16)


def solution(mesh):
    return jax.shard_map(
        shards,
        mesh=mesh,
        in_specs=(
            P("ctx", "mp"),
            P(None, "mp"),
            P(None, "mp"),
            P(),
            P(None, "mp"),
            P(None, "mp"),
            P(),
            P("mp"),
            P("mp"),
            P("mp"),
            P("mp"),
            P("mp", None),
            P(),
        ),
        out_specs=P("ctx", "mp"),
        check_vma=False,
    )
```

profile of v0, /device:TPU:24, one launch (start us, length us, event | category | flops | bytes accessed | tf_op | source)
XLA Modules:
  0.0 119.1 jit_solution(518911284680527722)
XLA Ops:
  1.0 2.0 %collective-permute-start.5 = (bf16[1056,128]{1,0:T(8,128)(2,1)S(1)}, bf16[1056,128]{1,0:T(8,128)(2,1)S(1)}, u32[]{:S(2)}, u32[]{:S(2)}) collective-permute-start(bf16[1056,128]{1,0:T(8,128)(2,1)S(1)} %slice.25.h0), channel_id=1, source_target_pairs={{0,1},{1,2},{2,3},{3,0},{4,5},{5,6},{6,7},{7,4},{8,9},{9,10},{10,1... | collective-permute-start | bytes 811016 | tf_op jit(solution)/shard_map/ppermute | solution.py:640
  4.7 1.3 %collective-permute-start = (bf16[16,128]{1,0:T(8,128)(2,1)S(1)}, bf16[16,128]{1,0:T(8,128)(2,1)S(1)}, u32[]{:S(2)}, u32[]{:S(2)}) collective-permute-start(bf16[16,128]{1,0:T(8,128)(2,1)S(1)} %get-tuple-element.173), channel_id=1, source_target_pairs={{0,4},{4,8},{8,12},{12,16},{16,20},{20,24},{24,28},{28,32},{32,36}... | collective-permute-start | bytes 12296 | tf_op jit(solution)/shard_map/ppermute | solution.py:665
  6.0 1.3 %collective-permute-start.1 = (bf16[16,128]{1,0:T(8,128)(2,1)S(1)}, bf16[16,128]{1,0:T(8,128)(2,1)S(1)}, u32[]{:S(2)}, u32[]{:S(2)}) collective-permute-start(bf16[16,128]{1,0:T(8,128)(2,1)S(1)} %get-tuple-element.174), channel_id=1, source_target_pairs={{4,0},{8,4},{12,8},{16,12},{20,16},{24,20},{28,24},{32,28},{36,32}... | collective-permute-start | bytes 12296 | tf_op jit(solution)/shard_map/ppermute | solution.py:666
  10.5 1.4 %convolution_convert_fusion.w_r = bf16[512,384]{1,0:T(8,128)(2,1)S(1)} fusion(s32[512]{0:T(512)S(1)} %get-tuple-element.180, bf16[512,128]{1,0:T(8,128)(2,1)S(1)} %get-tuple-element.177, bf16[512,256]{1,0:T(8,128)(2,1)} %param.16), kind=kOutput, calls=%fused_computation | convolution fusion | flops 202571776 | bytes 788480 | tf_op jit(solution)/shard_map/dot_general | solution.py:679
  13.8 3.2 %collective-permute-start.2 = (bf16[1088,128]{1,0:T(8,128)(2,1)S(1)}, bf16[1088,128]{1,0:T(8,128)(2,1)S(1)}, u32[]{:S(2)}, u32[]{:S(2)}) collective-permute-start(bf16[1088,128]{1,0:T(8,128)(2,1)S(1)} %pad_maximum_fusion.2.h0), channel_id=1, source_target_pairs={{0,1},{1,2},{2,3},{3,0},{4,5},{5,6},{6,7},{7,4},{8,9},{9,10},{10,1... | collective-permute-start | bytes 835592 | tf_op jit(solution)/shard_map/ppermute | solution.py:640
  17.0 1.5 %collective-permute-start.3 = (bf16[1088,128]{1,0:T(8,128)(2,1)S(1)}, bf16[1088,128]{1,0:T(8,128)(2,1)S(1)}, u32[]{:S(2)}, u32[]{:S(2)}) collective-permute-start(bf16[1088,128]{1,0:T(8,128)(2,1)S(1)} %pad_maximum_fusion.2.h0), channel_id=1, source_target_pairs={{0,2},{1,3},{2,0},{3,1},{4,6},{5,7},{6,4},{7,5},{8,10},{9,11},{10,... | collective-permute-start | bytes 835592 | tf_op jit(solution)/shard_map/ppermute | solution.py:640
  18.6 5.4 %local_states.2 = (bf16[1024,384]{1,0:T(8,128)(2,1)S(1)}, bf16[1024,384]{1,0:T(8,128)(2,1)S(1)}, f32[8,1024]{1,0:T(8,128)S(1)}, f32[8,1024]{1,0:T(8,128)S(1)}, f...) custom-call(s32[16]{0:T(128)S(1)} %copy-done.7, s32[4]{0:T(128)S(1)} %pad_add_fusion.meta, ...), custom_call_target="tpu_custom_call" | custom-call | flops 6144000000 | bytes 4096000 | tf_op jit(solution)/shard_map/local_states/pallas_call | solution.py:309
  24.0 5.7 %intra.3 = (bf16[1024,128]{1,0:T(8,128)(2,1)S(1)}, bf16[1024,128]{1,0:T(8,128)(2,1)S(1)}, f32[1024,256]{1,0:T(8,128)S(1)}, f32[1024,256]{1,0:T(8,128)S(1)}, f32[...) custom-call(s32[16]{0:T(128)S(1)} %copy-done.7, s32[4]{0:T(128)S(1)} %pad_add_fusion.meta, f32[4]{0:T(128)S(1)} %copy-done.8, ...), custom_call_target="tpu_custom_call" | custom-call | flops 5120000000 | bytes 5120000 | tf_op jit(solution)/shard_map/intra/pallas_call | solution.py:406
  29.8 4.2 %collective-permute-done.4.h3 = bf16[1088,128]{1,0:T(8,128)(2,1)S(1)} collective-permute-done((bf16[1088,128]{1,0:T(8,128)(2,1)S(1)}, bf16[1088,128]{1,0:T(8,128)(2,1)S(1)}, u32[]{:S(2)}, u32[]{:S(2)}) %collective-permute-start.4) | collective-permute-done | bytes 278560 | tf_op jit(solution)/shard_map/ppermute | solution.py:640
  33.9 5.7 %local_states.3 = (bf16[1024,384]{1,0:T(8,128)(2,1)S(1)}, bf16[1024,384]{1,0:T(8,128)(2,1)S(1)}, f32[8,1024]{1,0:T(8,128)S(1)}, f32[8,1024]{1,0:T(8,128)S(1)}, f...) custom-call(s32[16]{0:T(128)S(1)} %copy-done.7, ...), custom_call_target="tpu_custom_call" | custom-call | flops 6144000000 | bytes 4096000 | tf_op jit(solution)/shard_map/local_states/pallas_call | solution.py:309
  39.6 3.6 %collective-permute-start.10 = (bf16[80,256]{1,0:T(8,128)(2,1)S(1)}, bf16[80,256]{1,0:T(8,128)(2,1)S(1)}, u32[]{:S(2)}, u32[]{:S(2)}) collective-permute-start(bf16[80,256]{1,0:T(8,128)(2,1)S(1)} %get-tuple-element.108), channel_id=1, source_target_pairs={{0,12},{4,0},{8,4},{12,8},{16,28},{20,16},{24,20},{28,24},{32,44},... | collective-permute-start | bytes 122888 | tf_op jit(solution)/shard_map/ppermute | solution.py:719
  44.1 3.1 %intra.4 = (bf16[1024,128]{1,0:T(8,128)(2,1)S(1)}, bf16[1024,128]{1,0:T(8,128)(2,1)S(1)}, f32[1024,256]{1,0:T(8,128)S(1)}, f32[1024,256]{1,0:T(8,128)S(1)}, f32[...) custom-call(s32[16]{0:T(128)S(1)} %copy-done.7, s32[4]{0:T(128)S(1)} %pad_add_fusion.meta, f32[4]{0:T(128)S(1)} %copy-done.8, ...), custom_call_target="tpu_custom_call" | custom-call | flops 2560000000 | bytes 2560000 | tf_op jit(solution)/shard_map/intra/pallas_call | solution.py:406
  48.1 4.3 %collective-permute-start.11 = (bf16[80,256]{1,0:T(8,128)(2,1)S(1)}, bf16[80,256]{1,0:T(8,128)(2,1)S(1)}, u32[]{:S(2)}, u32[]{:S(2)}) collective-permute-start(bf16[80,256]{1,0:T(8,128)(2,1)S(1)} %get-tuple-element.122.own), channel_id=1, source_target_pairs={{0,16},{4,20},{8,24},{12,28},{16,32},{20,36},{24,40},{28,44},{32,4... | collective-permute-start | bytes 122888 | tf_op jit(solution)/shard_map/ppermute | solution.py:719
  52.4 2.5 %collective-permute-start.12 = (bf16[80,256]{1,0:T(8,128)(2,1)S(1)}, bf16[80,256]{1,0:T(8,128)(2,1)S(1)}, u32[]{:S(2)}, u32[]{:S(2)}) collective-permute-start(bf16[80,256]{1,0:T(8,128)(2,1)S(1)} %get-tuple-element.122.own), channel_id=1, source_target_pairs={{0,32},{4,36},{8,40},{12,44},{16,48},{20,52},{24,56},{28,60},{32,0... | collective-permute-start | bytes 122888 | tf_op jit(solution)/shard_map/ppermute | solution.py:719
  54.9 2.8 %collective-permute-start.13 = (bf16[80,256]{1,0:T(8,128)(2,1)S(1)}, bf16[80,256]{1,0:T(8,128)(2,1)S(1)}, u32[]{:S(2)}, u32[]{:S(2)}) collective-permute-start(bf16[80,256]{1,0:T(8,128)(2,1)S(1)} %get-tuple-element.122.own), channel_id=1, source_target_pairs={{0,48},{4,52},{8,56},{12,60},{16,0},{20,4},{24,8},{28,12},{32,16},... | collective-permute-start | bytes 122888 | tf_op jit(solution)/shard_map/ppermute | solution.py:719
  57.7 3.1 %intra.5 = (bf16[1024,128]{1,0:T(8,128)(2,1)S(1)}, bf16[1024,128]{1,0:T(8,128)(2,1)S(1)}, f32[1024,256]{1,0:T(8,128)S(1)}, f32[1024,256]{1,0:T(8,128)S(1)}, f32[...) custom-call(s32[16]{0:T(128)S(1)} %copy-done.7, ...), custom_call_target="tpu_custom_call", output_to_operand_aliasing={{0}: (15, {}), {1}: (16, {}), {2}: (17, {}), {3}: (18, {}),... | custom-call | flops 2560000000 | bytes 2560000 | tf_op jit(solution)/shard_map/intra/pallas_call | solution.py:406
  61.7 1.6 %collective-permute-start.14 = (bf16[80,256]{1,0:T(8,128)(2,1)S(1)}, bf16[80,256]{1,0:T(8,128)(2,1)S(1)}, u32[]{:S(2)}, u32[]{:S(2)}) collective-permute-start(bf16[80,256]{1,0:T(8,128)(2,1)S(1)} %get-tuple-element.147), channel_id=1, source_target_pairs={{0,64},{4,68},{8,72},{12,76},{16,80},{20,84},{24,88},{28,92},{32,9... | collective-permute-start | bytes 122888 | tf_op jit(solution)/shard_map/ppermute | solution.py:719
  63.3 2.7 %collective-permute-start.15 = (bf16[80,256]{1,0:T(8,128)(2,1)S(1)}, bf16[80,256]{1,0:T(8,128)(2,1)S(1)}, u32[]{:S(2)}, u32[]{:S(2)}) collective-permute-start(bf16[80,256]{1,0:T(8,128)(2,1)S(1)} %get-tuple-element.147), channel_id=1, source_target_pairs={{0,128},{4,132},{8,136},{12,140},{16,144},{20,148},{24,152},{28,15... | collective-permute-start | bytes 122888 | tf_op jit(solution)/shard_map/ppermute | solution.py:719
  66.0 1.4 %collective-permute-start.16 = (bf16[80,256]{1,0:T(8,128)(2,1)S(1)}, bf16[80,256]{1,0:T(8,128)(2,1)S(1)}, u32[]{:S(2)}, u32[]{:S(2)}) collective-permute-start(bf16[80,256]{1,0:T(8,128)(2,1)S(1)} %get-tuple-element.147), channel_id=1, source_target_pairs={{0,192},{4,196},{8,200},{12,204},{16,208},{20,212},{24,216},{28,22... | collective-permute-start | bytes 122888 | tf_op jit(solution)/shard_map/ppermute | solution.py:719
  67.5 1.3 %collective-permute-done.15.r2 = bf16[80,256]{1,0:T(8,128)(2,1)S(1)} collective-permute-done((bf16[80,256]{1,0:T(8,128)(2,1)S(1)}, bf16[80,256]{1,0:T(8,128)(2,1)S(1)}, u32[]{:S(2)}, u32[]{:S(2)}) %collective-permute-start.15) | collective-permute-done | bytes 40992 | tf_op jit(solution)/shard_map/ppermute | solution.py:719
  68.8 1.2 %collective-permute-done.16.r3 = bf16[80,256]{1,0:T(8,128)(2,1)S(1)} collective-permute-done((bf16[80,256]{1,0:T(8,128)(2,1)S(1)}, bf16[80,256]{1,0:T(8,128)(2,1)S(1)}, u32[]{:S(2)}, u32[]{:S(2)}) %collective-permute-start.16) | collective-permute-done | bytes 40992 | tf_op jit(solution)/shard_map/ppermute | solution.py:719
  71.6 1.4 %collective-permute-start.19 = (bf16[64,256]{1,0:T(8,128)(2,1)S(1)}, bf16[64,256]{1,0:T(8,128)(2,1)S(1)}, u32[]{:S(2)}, u32[]{:S(2)}) collective-permute-start(bf16[64,256]{1,0:T(8,128)(2,1)S(1)} %get-tuple-element.155), channel_id=1, source_target_pairs={{0,12},{4,0},{8,4},{12,8},{16,28},{20,16},{24,20},{28,24},{32,44},... | collective-permute-start | bytes 98312 | tf_op jit(solution)/shard_map/ppermute | solution.py:719
  74.9 2.8 %gate.2 = (bf16[2048,256]{1,0:T(8,128)(2,1)S(1)}, bf16[2048,256]{1,0:T(8,128)(2,1)S(1)}, f32[2,2048]{1,0:T(2,128)S(1)}) custom-call(s32[4]{0:T(128)S(1)} %pad_add_fusion.meta, bf16[1024,128]{1,0:T(8,128)(2,1)S(1)} %get-tuple-element.156.c_f, bf16[1024,128]{1,0:T(8,128)(2,1)S(1)} %get-tuple-element.157.c_r, f32[1024,256]{1,0:T(8,128)S(1)} %get-tuple-element.158.y_f, ...), custom_call_target="tpu_custom_call" | custom-call | flops 614400000 | bytes 6144000 | tf_op jit(solution)/shard_map/gate/pallas_call | solution.py:576
  77.7 2.8 %gate.3 = (bf16[2048,256]{1,0:T(8,128)(2,1)S(1)}, bf16[2048,256]{1,0:T(8,128)(2,1)S(1)}, f32[2,2048]{1,0:T(2,128)S(1)}) custom-call(s32[4]{0:T(128)S(1)} %pad_add_fusion.meta, bf16[1024,128]{1,0:T(8,128)(2,1)S(1)} %get-tuple-element.135.c_f, ...), custom_call_target="tpu_custom_call", output_to_operand_aliasing={{0}: (16, {}), {1}: (17, {}), {2}: (18, {})} | custom-call | flops 614400000 | bytes 6144000 | tf_op jit(solution)/shard_map/gate/pallas_call | solution.py:576
  81.3 1.7 %collective-permute-start.21 = (f32[2,2048]{1,0:T(2,128)S(1)}, f32[2,2048]{1,0:T(2,128)S(1)}, u32[]{:S(2)}, u32[]{:S(2)}) collective-permute-start(f32[2,2048]{1,0:T(2,128)S(1)} %get-tuple-element.168.s0), channel_id=1, source_target_pairs={{0,2},{1,3},{2,0},{3,1},{4,6},{5,7},{6,4},{7,5},{8,10},{9,11},{10,... | collective-permute-start | bytes 49160 | tf_op jit(solution)/shard_map/ppermute | solution.py:640
  84.5 2.0 %collective-permute-done.21.s2 = f32[2,2048]{1,0:T(2,128)S(1)} collective-permute-done((f32[2,2048]{1,0:T(2,128)S(1)}, f32[2,2048]{1,0:T(2,128)S(1)}, u32[]{:S(2)}, u32[]{:S(2)}) %collective-permute-start.21) | collective-permute-done | bytes 16416 | tf_op jit(solution)/shard_map/ppermute | solution.py:640
  86.5 1.5 %collective-permute-done.22.s3 = f32[2,2048]{1,0:T(2,128)S(1)} collective-permute-done((f32[2,2048]{1,0:T(2,128)S(1)}, f32[2,2048]{1,0:T(2,128)S(1)}, u32[]{:S(2)}, u32[]{:S(2)}) %collective-permute-start.22) | collective-permute-done | bytes 16416 | tf_op jit(solution)/shard_map/ppermute | solution.py:640
  88.0 3.2 %project_out.1 = (f32[2048,128]{1,0:T(8,128)S(1)}, bf16[2048,128]{1,0:T(8,128)(2,1)S(1)}, bf16[2048,128]{1,0:T(8,128)(2,1)S(1)}, bf16[2048,128]{1,0:T(8,128)(2,1)S(1)}) custom-call(bf16[2048,256]{1,0:T(8,128)(2,1)S(1)} %get-tuple-element.166.g_f, bf16[2048,256]{1,0:T(8,128)(2,1)S(1)} %get-tuple-element.167.g_r, f32[2,2048]{1,0:T(2,128)S(1)} %get-tuple-element.168.s0, ...), custom_call_target="tpu_custom_call" | custom-call | flops 2048000000 | bytes 6144000 | tf_op jit(solution)/shard_map/project_out/pallas_call | solution.py:619
  91.2 1.2 collective-permute-start.23
  93.4 12.8 %collective-permute-done.23 = bf16[2048,128]{1,0:T(8,128)(2,1)S(1)} collective-permute-done((bf16[2048,128]{1,0:T(8,128)(2,1)S(1)}, bf16[2048,128]{1,0:T(8,128)(2,1)S(1)}, u32[]{:S(2)}, u32[]{:S(2)}) %collective-permute-start.23) | collective-permute-done | bytes 524320 | tf_op jit(solution)/shard_map/ppermute | solution.py:640
  106.2 2.7 %collective-permute-done.24 = bf16[2048,128]{1,0:T(8,128)(2,1)S(1)} collective-permute-done((bf16[2048,128]{1,0:T(8,128)(2,1)S(1)}, bf16[2048,128]{1,0:T(8,128)(2,1)S(1)}, u32[]{:S(2)}, u32[]{:S(2)}) %collective-permute-start.24) | collective-permute-done | bytes 524320 | tf_op jit(solution)/shard_map/ppermute | solution.py:640
  108.8 9.2 %collective-permute-done.25 = bf16[2048,128]{1,0:T(8,128)(2,1)S(1)} collective-permute-done((bf16[2048,128]{1,0:T(8,128)(2,1)S(1)}, bf16[2048,128]{1,0:T(8,128)(2,1)S(1)}, u32[]{:S(2)}, u32[]{:S(2)}) %collective-permute-start.25) | collective-permute-done | bytes 524320 | tf_op jit(solution)/shard_map/ppermute | solution.py:640
  (75 shorter events, 18.0 us)
Async XLA Ops:
  0.0 73.0 %copy-start = (bf16[256,512]{1,0:T(8,128)(2,1)S(1)}, bf16[256,512]{1,0:T(8,128)(2,1)}, u32[]{:S(2)}) copy-start(bf16[256,512]{1,0:T(8,128)(2,1)} %param.26) | copy-start | bytes 786436
  0.0 12.0 %copy-start.11 = (bf16[512,256]{1,0:T(8,128)(2,1)S(1)}, bf16[512,256]{1,0:T(8,128)(2,1)}, u32[]{:S(2)}) copy-start(bf16[512,256]{1,0:T(8,128)(2,1)} %param.16) | copy-start | bytes 786436
  1.0 11.5 %copy-start.12 = (bf16[512,256]{1,0:T(8,128)(2,1)S(1)}, bf16[512,256]{1,0:T(8,128)(2,1)}, u32[]{:S(2)}) copy-start(bf16[512,256]{1,0:T(8,128)(2,1)} %param.17) | copy-start | bytes 786436
  1.0 17.4 %collective-permute-start.5 = (bf16[1056,128]{1,0:T(8,128)(2,1)S(1)}, bf16[1056,128]{1,0:T(8,128)(2,1)S(1)}, u32[]{:S(2)}, u32[]{:S(2)}) collective-permute-start(bf16[1056,128]{1,0:T(8,128)(2,1)S(1)} %slice.25.h0), channel_id=1, source_target_pairs={{0,1},{1,2},{2,3},{3,0},{4,5},{5,6},{6,7},{7,4},{8,9},{9,10},{10,1... | collective-permute-start | bytes 811016 | tf_op jit(solution)/shard_map/ppermute | solution.py:640
  3.1 15.4 %collective-permute-start.6 = (bf16[1056,128]{1,0:T(8,128)(2,1)S(1)}, bf16[1056,128]{1,0:T(8,128)(2,1)S(1)}, u32[]{:S(2)}, u32[]{:S(2)}) collective-permute-start(bf16[1056,128]{1,0:T(8,128)(2,1)S(1)} %slice.25.h0), channel_id=1, source_target_pairs={{0,2},{1,3},{2,0},{3,1},{4,6},{5,7},{6,4},{7,5},{8,10},{9,11},{10,... | collective-permute-start | bytes 811016 | tf_op jit(solution)/shard_map/ppermute | solution.py:640
  3.9 14.6 %collective-permute-start.7 = (bf16[1056,128]{1,0:T(8,128)(2,1)S(1)}, bf16[1056,128]{1,0:T(8,128)(2,1)S(1)}, u32[]{:S(2)}, u32[]{:S(2)}) collective-permute-start(bf16[1056,128]{1,0:T(8,128)(2,1)S(1)} %slice.25.h0), channel_id=1, source_target_pairs={{0,3},{1,0},{2,1},{3,2},{4,7},{5,4},{6,5},{7,6},{8,11},{9,8},{10,9... | collective-permute-start | bytes 811016 | tf_op jit(solution)/shard_map/ppermute | solution.py:640
  4.7 9.0 %collective-permute-start = (bf16[16,128]{1,0:T(8,128)(2,1)S(1)}, bf16[16,128]{1,0:T(8,128)(2,1)S(1)}, u32[]{:S(2)}, u32[]{:S(2)}) collective-permute-start(bf16[16,128]{1,0:T(8,128)(2,1)S(1)} %get-tuple-element.173), channel_id=1, source_target_pairs={{0,4},{4,8},{8,12},{12,16},{16,20},{20,24},{24,28},{28,32},{32,36}... | collective-permute-start | bytes 12296 | tf_op jit(solution)/shard_map/ppermute | solution.py:665
  6.0 7.7 %collective-permute-start.1 = (bf16[16,128]{1,0:T(8,128)(2,1)S(1)}, bf16[16,128]{1,0:T(8,128)(2,1)S(1)}, u32[]{:S(2)}, u32[]{:S(2)}) collective-permute-start(bf16[16,128]{1,0:T(8,128)(2,1)S(1)} %get-tuple-element.174), channel_id=1, source_target_pairs={{4,0},{8,4},{12,8},{16,12},{20,16},{24,20},{28,24},{32,28},{36,32}... | collective-permute-start | bytes 12296 | tf_op jit(solution)/shard_map/ppermute | solution.py:666
  13.8 10.3 %copy-start.8 = (f32[4]{0:T(128)S(1)}, f32[4]{0:T(128)}, u32[]{:S(2)}) copy-start(f32[4]{0:T(128)} %skip_gain.5) | copy-start | bytes 52
  13.8 16.0 %collective-permute-start.2 = (bf16[1088,128]{1,0:T(8,128)(2,1)S(1)}, bf16[1088,128]{1,0:T(8,128)(2,1)S(1)}, u32[]{:S(2)}, u32[]{:S(2)}) collective-permute-start(bf16[1088,128]{1,0:T(8,128)(2,1)S(1)} %pad_maximum_fusion.2.h0), channel_id=1, source_target_pairs={{0,1},{1,2},{2,3},{3,0},{4,5},{5,6},{6,7},{7,4},{8,9},{9,10},{10,1... | collective-permute-start | bytes 835592 | tf_op jit(solution)/shard_map/ppermute | solution.py:640
  17.0 12.8 %collective-permute-start.3 = (bf16[1088,128]{1,0:T(8,128)(2,1)S(1)}, bf16[1088,128]{1,0:T(8,128)(2,1)S(1)}, u32[]{:S(2)}, u32[]{:S(2)}) collective-permute-start(bf16[1088,128]{1,0:T(8,128)(2,1)S(1)} %pad_maximum_fusion.2.h0), channel_id=1, source_target_pairs={{0,2},{1,3},{2,0},{3,1},{4,6},{5,7},{6,4},{7,5},{8,10},{9,11},{10,... | collective-permute-start | bytes 835592 | tf_op jit(solution)/shard_map/ppermute | solution.py:640
  18.4 15.5 %collective-permute-start.4 = (bf16[1088,128]{1,0:T(8,128)(2,1)S(1)}, bf16[1088,128]{1,0:T(8,128)(2,1)S(1)}, u32[]{:S(2)}, u32[]{:S(2)}) collective-permute-start(bf16[1088,128]{1,0:T(8,128)(2,1)S(1)} %pad_maximum_fusion.2.h0), channel_id=1, source_target_pairs={{0,3},{1,0},{2,1},{3,2},{4,7},{5,4},{6,5},{7,6},{8,11},{9,8},{10,9... | collective-permute-start | bytes 835592 | tf_op jit(solution)/shard_map/ppermute | solution.py:640
  39.6 7.7 %collective-permute-start.10 = (bf16[80,256]{1,0:T(8,128)(2,1)S(1)}, bf16[80,256]{1,0:T(8,128)(2,1)S(1)}, u32[]{:S(2)}, u32[]{:S(2)}) collective-permute-start(bf16[80,256]{1,0:T(8,128)(2,1)S(1)} %get-tuple-element.108), channel_id=1, source_target_pairs={{0,12},{4,0},{8,4},{12,8},{16,28},{20,16},{24,20},{28,24},{32,44},... | collective-permute-start | bytes 122888 | tf_op jit(solution)/shard_map/ppermute | solution.py:719
  43.1 4.1 %collective-permute-start.8 = (bf16[80,256]{1,0:T(8,128)(2,1)S(1)}, bf16[80,256]{1,0:T(8,128)(2,1)S(1)}, u32[]{:S(2)}, u32[]{:S(2)}) collective-permute-start(bf16[80,256]{1,0:T(8,128)(2,1)S(1)} %get-tuple-element.106), channel_id=1, source_target_pairs={{0,4},{4,8},{8,12},{12,0},{16,20},{20,24},{24,28},{28,16},{32,36},... | collective-permute-start | bytes 122888 | tf_op jit(solution)/shard_map/ppermute | solution.py:719
  43.1 4.3 %collective-permute-start.9 = (bf16[80,256]{1,0:T(8,128)(2,1)S(1)}, bf16[80,256]{1,0:T(8,128)(2,1)S(1)}, u32[]{:S(2)}, u32[]{:S(2)}) collective-permute-start(bf16[80,256]{1,0:T(8,128)(2,1)S(1)} %get-tuple-element.107), channel_id=1, source_target_pairs={{0,8},{4,12},{8,0},{12,4},{16,24},{20,28},{24,16},{28,20},{32,40},... | collective-permute-start | bytes 122888 | tf_op jit(solution)/shard_map/ppermute | solution.py:719
  48.0 26.9 %copy-start.2 = (f32[256]{0:T(256)S(1)}, f32[256]{0:T(256)}, u32[]{:S(2)}) copy-start(f32[256]{0:T(256)} %param.25) | copy-start | bytes 3076
  48.1 12.8 %collective-permute-start.11 = (bf16[80,256]{1,0:T(8,128)(2,1)S(1)}, bf16[80,256]{1,0:T(8,128)(2,1)S(1)}, u32[]{:S(2)}, u32[]{:S(2)}) collective-permute-start(bf16[80,256]{1,0:T(8,128)(2,1)S(1)} %get-tuple-element.122.own), channel_id=1, source_target_pairs={{0,16},{4,20},{8,24},{12,28},{16,32},{20,36},{24,40},{28,44},{32,4... | collective-permute-start | bytes 122888 | tf_op jit(solution)/shard_map/ppermute | solution.py:719
  52.4 8.7 %collective-permute-start.12 = (bf16[80,256]{1,0:T(8,128)(2,1)S(1)}, bf16[80,256]{1,0:T(8,128)(2,1)S(1)}, u32[]{:S(2)}, u32[]{:S(2)}) collective-permute-start(bf16[80,256]{1,0:T(8,128)(2,1)S(1)} %get-tuple-element.122.own), channel_id=1, source_target_pairs={{0,32},{4,36},{8,40},{12,44},{16,48},{20,52},{24,56},{28,60},{32,0... | collective-permute-start | bytes 122888 | tf_op jit(solution)/shard_map/ppermute | solution.py:719
  54.9 6.2 %collective-permute-start.13 = (bf16[80,256]{1,0:T(8,128)(2,1)S(1)}, bf16[80,256]{1,0:T(8,128)(2,1)S(1)}, u32[]{:S(2)}, u32[]{:S(2)}) collective-permute-start(bf16[80,256]{1,0:T(8,128)(2,1)S(1)} %get-tuple-element.122.own), channel_id=1, source_target_pairs={{0,48},{4,52},{8,56},{12,60},{16,0},{20,4},{24,8},{28,12},{32,16},... | collective-permute-start | bytes 122888 | tf_op jit(solution)/shard_map/ppermute | solution.py:719
  61.7 5.8 %collective-permute-start.14 = (bf16[80,256]{1,0:T(8,128)(2,1)S(1)}, bf16[80,256]{1,0:T(8,128)(2,1)S(1)}, u32[]{:S(2)}, u32[]{:S(2)}) collective-permute-start(bf16[80,256]{1,0:T(8,128)(2,1)S(1)} %get-tuple-element.147), channel_id=1, source_target_pairs={{0,64},{4,68},{8,72},{12,76},{16,80},{20,84},{24,88},{28,92},{32,9... | collective-permute-start | bytes 122888 | tf_op jit(solution)/shard_map/ppermute | solution.py:719
  63.3 5.5 %collective-permute-start.15 = (bf16[80,256]{1,0:T(8,128)(2,1)S(1)}, bf16[80,256]{1,0:T(8,128)(2,1)S(1)}, u32[]{:S(2)}, u32[]{:S(2)}) collective-permute-start(bf16[80,256]{1,0:T(8,128)(2,1)S(1)} %get-tuple-element.147), channel_id=1, source_target_pairs={{0,128},{4,132},{8,136},{12,140},{16,144},{20,148},{24,152},{28,15... | collective-permute-start | bytes 122888 | tf_op jit(solution)/shard_map/ppermute | solution.py:719
  66.0 4.0 %collective-permute-start.16 = (bf16[80,256]{1,0:T(8,128)(2,1)S(1)}, bf16[80,256]{1,0:T(8,128)(2,1)S(1)}, u32[]{:S(2)}, u32[]{:S(2)}) collective-permute-start(bf16[80,256]{1,0:T(8,128)(2,1)S(1)} %get-tuple-element.147), channel_id=1, source_target_pairs={{0,192},{4,196},{8,200},{12,204},{16,208},{20,212},{24,216},{28,22... | collective-permute-start | bytes 122888 | tf_op jit(solution)/shard_map/ppermute | solution.py:719
  70.6 3.4 %collective-permute-start.17 = (bf16[64,256]{1,0:T(8,128)(2,1)S(1)}, bf16[64,256]{1,0:T(8,128)(2,1)S(1)}, u32[]{:S(2)}, u32[]{:S(2)}) collective-permute-start(bf16[64,256]{1,0:T(8,128)(2,1)S(1)} %get-tuple-element.153), channel_id=1, source_target_pairs={{0,4},{4,8},{8,12},{12,0},{16,20},{20,24},{24,28},{28,16},{32,36},... | collective-permute-start | bytes 98312 | tf_op jit(solution)/shard_map/ppermute | solution.py:719
  70.7 4.2 %collective-permute-start.18 = (bf16[64,256]{1,0:T(8,128)(2,1)S(1)}, bf16[64,256]{1,0:T(8,128)(2,1)S(1)}, u32[]{:S(2)}, u32[]{:S(2)}) collective-permute-start(bf16[64,256]{1,0:T(8,128)(2,1)S(1)} %get-tuple-element.154), channel_id=1, source_target_pairs={{0,8},{4,12},{8,0},{12,4},{16,24},{20,28},{24,16},{28,20},{32,40},... | collective-permute-start | bytes 98312 | tf_op jit(solution)/shard_map/ppermute | solution.py:719
  71.6 3.3 %collective-permute-start.19 = (bf16[64,256]{1,0:T(8,128)(2,1)S(1)}, bf16[64,256]{1,0:T(8,128)(2,1)S(1)}, u32[]{:S(2)}, u32[]{:S(2)}) collective-permute-start(bf16[64,256]{1,0:T(8,128)(2,1)S(1)} %get-tuple-element.155), channel_id=1, source_target_pairs={{0,12},{4,0},{8,4},{12,8},{16,28},{20,16},{24,20},{28,24},{32,44},... | collective-permute-start | bytes 98312 | tf_op jit(solution)/shard_map/ppermute | solution.py:719
  77.7 10.3 %copy-start.9 = (bf16[16,256]{1,0:T(8,128)(2,1)S(1)}, bf16[16,256]{1,0:T(8,128)(2,1)}, u32[]{:S(2)}) copy-start(bf16[16,256]{1,0:T(8,128)(2,1)} %constant.116.clone.spread) | copy-start | bytes 24580
  80.6 4.0 %collective-permute-start.20 = (f32[2,2048]{1,0:T(2,128)S(1)}, f32[2,2048]{1,0:T(2,128)S(1)}, u32[]{:S(2)}, u32[]{:S(2)}) collective-permute-start(f32[2,2048]{1,0:T(2,128)S(1)} %get-tuple-element.168.s0), channel_id=1, source_target_pairs={{0,1},{1,2},{2,3},{3,0},{4,5},{5,6},{6,7},{7,4},{8,9},{9,10},{10,1... | collective-permute-start | bytes 49160 | tf_op jit(solution)/shard_map/ppermute | solution.py:640
  81.3 5.2 %collective-permute-start.21 = (f32[2,2048]{1,0:T(2,128)S(1)}, f32[2,2048]{1,0:T(2,128)S(1)}, u32[]{:S(2)}, u32[]{:S(2)}) collective-permute-start(f32[2,2048]{1,0:T(2,128)S(1)} %get-tuple-element.168.s0), channel_id=1, source_target_pairs={{0,2},{1,3},{2,0},{3,1},{4,6},{5,7},{6,4},{7,5},{8,10},{9,11},{10,... | collective-permute-start | bytes 49160 | tf_op jit(solution)/shard_map/ppermute | solution.py:640
  83.0 4.9 %collective-permute-start.22 = (f32[2,2048]{1,0:T(2,128)S(1)}, f32[2,2048]{1,0:T(2,128)S(1)}, u32[]{:S(2)}, u32[]{:S(2)}) collective-permute-start(f32[2,2048]{1,0:T(2,128)S(1)} %get-tuple-element.168.s0), channel_id=1, source_target_pairs={{0,3},{1,0},{2,1},{3,2},{4,7},{5,4},{6,5},{7,6},{8,11},{9,8},{10,9... | collective-permute-start | bytes 49160 | tf_op jit(solution)/shard_map/ppermute | solution.py:640
  91.2 14.9 %collective-permute-start.23 = (bf16[2048,128]{1,0:T(8,128)(2,1)S(1)}, bf16[2048,128]{1,0:T(8,128)(2,1)S(1)}, u32[]{:S(2)}, u32[]{:S(2)}) collective-permute-start(bf16[2048,128]{1,0:T(8,128)(2,1)S(1)} %get-tuple-element.170), channel_id=1, source_target_pairs={{0,1},{1,2},{2,3},{3,0},{4,5},{5,6},{6,7},{7,4},{8,9},{9,10},{10,1... | collective-permute-start | bytes 1572872 | tf_op jit(solution)/shard_map/ppermute | solution.py:640
  92.4 16.4 %collective-permute-start.24 = (bf16[2048,128]{1,0:T(8,128)(2,1)S(1)}, bf16[2048,128]{1,0:T(8,128)(2,1)S(1)}, u32[]{:S(2)}, u32[]{:S(2)}) collective-permute-start(bf16[2048,128]{1,0:T(8,128)(2,1)S(1)} %get-tuple-element.171), channel_id=1, source_target_pairs={{0,2},{1,3},{2,0},{3,1},{4,6},{5,7},{6,4},{7,5},{8,10},{9,11},{10,... | collective-permute-start | bytes 1572872 | tf_op jit(solution)/shard_map/ppermute | solution.py:640
  93.3 24.7 %collective-permute-start.25 = (bf16[2048,128]{1,0:T(8,128)(2,1)S(1)}, bf16[2048,128]{1,0:T(8,128)(2,1)S(1)}, u32[]{:S(2)}, u32[]{:S(2)}) collective-permute-start(bf16[2048,128]{1,0:T(8,128)(2,1)S(1)} %get-tuple-element.172), channel_id=1, source_target_pairs={{0,3},{1,0},{2,1},{3,2},{4,7},{5,4},{6,5},{7,6},{8,11},{9,8},{10,9... | collective-permute-start | bytes 1572872 | tf_op jit(solution)/shard_map/ppermute | solution.py:640
  (7 other events, 37.6 us)
where the time goes:
time: 120 us; the launch traced here: 119 us
  waiting for transfers between devices  37.9 us (32%)
  starting transfers between devices  37.2 us (31%)
  Pallas kernels  33.7 us (28%)
  matrix products  5.74 us (5%)
  local copies, waits for them, and re-layouts  2.83 us (2%)
  other arithmetic  1.22 us (1%)
    ppermute x12, waiting for transfers between devices, around(): lax.ppermute(array, axis, [(i, (i + shift) % count) for i in range(count)])  33.4 us
    ppermute x12, starting transfers between devices, moved(): lax.ppermute(a, 'ctx', digit_perm(n_ctx, stride, s))  22.3 us
    ppermute x12, starting transfers between devices, around(): lax.ppermute(array, axis, [(i, (i + shift) % count) for i in range(count)])  12.3 us
    pallas_call x3, Pallas kernels, intra(): pl.pallas_call(functools.partial(k2_body, chunk, base, len(before)), grid...  11.9 us
    pallas_call x2, Pallas kernels, local_states(): pl.pallas_call(functools.partial(k1_body, chunk), grid=(HERE,), in_specs=...  11.1 us
    pallas_call x2, Pallas kernels, gate(): pl.pallas_call(k3_body, grid=(HERE,), in_specs=[SMEM, c_in, c_in, y_in, y...  5.61 us
    ppermute x12, waiting for transfers between devices, moved(): lax.ppermute(a, 'ctx', digit_perm(n_ctx, stride, s))  4.56 us
    pallas_call x1, Pallas kernels, project_out(): pl.pallas_call(k4_body, grid=(n,), in_specs=[g_in, g_in] + [s_in] * 4 + [...  3.24 us
  transfers between devices with their start and end apart: 26, of which 13 were waited for; matrix products, arithmetic and copies ran while one was open for 6% of the time, Pallas kernels for 15%

commit v1 on v0

--- a/solution.py
+++ b/solution.py
@@ -608,24 +608,113 @@
         ref[...] = part.astype(ref.dtype)
 
 
-def project_out(g_f, g_r, sums, w_f, w_r, spread):
-    m = g_f.shape[0]
-    n = m // BLOCK
-    g_in = pl.BlockSpec((BLOCK, INNER), lambda g: (g, 0))
-    s_in = pl.BlockSpec((2, BLOCK), lambda g: (0, g))
-    o = pl.BlockSpec(
-        (BLOCK, 128), lambda g: (jnp.where(g < HERE, block_of(0, g), block_of(1, g - HERE)), 0)
-    )
+def project_out(half, kinds, g_f, g_r, sums, w_f, w_r, spread):
+    m = HERE * BLOCK
+
+    def at(g):
+        return jnp.where(g < 2, g + 4, g - 2) if half == 0 else jnp.where(g < 2, g + 2, g + 4)
+
+    g_in = pl.BlockSpec((BLOCK, INNER), lambda g: (at(g), 0))
+    s_in = pl.BlockSpec((2, BLOCK), lambda g: (0, at(g)))
+    o = pl.BlockSpec((BLOCK, 128), lambda g: (g, 0))
     return pl.pallas_call(
         k4_body,
-        grid=(n,),
+        grid=(HERE,),
         in_specs=[g_in, g_in] + [s_in] * 4 + [whole(w_f.shape), whole(w_r.shape), whole(spread.shape)],
         out_specs=[o] * 4,
-        out_shape=[jax.ShapeDtypeStruct((m, 128), f32)] + [jax.ShapeDtypeStruct((m, 128), bf16)] * 3,
+        out_shape=[jax.ShapeDtypeStruct((m, 128), kind) for kind in kinds],
         compiler_params=params(16),
         cost_estimate=cost(m * 1e6, m * 3000),
         name="project_out",
     )(g_f, g_r, *sums, w_f, w_r, spread)
+
+
+def join_body(a1, b1, a2, b2, o1, o2):
+    o1[...] = (a1[...] + b1[...].astype(f32)).astype(bf16)
+    o2[...] = (a2[...] + b2[...].astype(f32)).astype(bf16)
+
+
+def join_shares(a1, b1, a2, b2):
+    arrays = (a1, b1, a2, b2)
+    shapes = [jax.ShapeDtypeStruct(a1.shape, bf16)] * 2
+    return pl.pallas_call(
+        join_body,
+        grid=(1,),
+        in_specs=[whole(a.shape) for a in arrays],
+        out_specs=[whole(a.shape) for a in shapes],
+        out_shape=shapes,
+        compiler_params=params(8),
+        cost_estimate=cost(1e6, 3e6),
+        name="join_shares",
+    )(*arrays)
+
+
+def last_body(a0, a1, a2, b0, b1, b2, out):
+    for k, (own, one, other) in enumerate(((a0, a1, a2), (b0, b1, b2))):
+        @pl.when(pl.program_id(0) == k)
+        def _():
+            out[...] = (own[...] + one[...].astype(f32) + other[...].astype(f32)).astype(bf16)
+
+
+def last_sum(*arrays):
+    m = HERE * BLOCK
+    return pl.pallas_call(
+        last_body,
+        grid=(2,),
+        in_specs=[whole(a.shape) for a in arrays],
+        out_specs=pl.BlockSpec((m, 128), lambda g: (g, 0)),
+        out_shape=jax.ShapeDtypeStruct((2 * m, 128), bf16),
+        compiler_params=params(8),
+        cost_estimate=cost(1e6, 3e6),
+        name="last_sum",
+    )(*arrays)
+
+
+def orders(mp, n_mp, width):
+    here = width // n_mp
+    shape = (width, width)
+    row = lax.broadcasted_iota(jnp.int32, shape, 0)
+    col = lax.broadcasted_iota(jnp.int32, shape, 1)
+    place = lax.rem(mp - row // here + n_mp, n_mp) * here + lax.rem(row, here)
+    goal = lax.rem(mp + col // here, n_mp) * here + lax.rem(col, here)
+    return [
+        keep.astype(f32).astype(bf16)
+        for keep in (place == col, width - 1 - place == col, goal == row, width - 1 - goal == row)
+    ]
+
+
+def prepare_1_body(n_mp, mp, w_x, w_bc, w_dt, o_f, o_r, o_dt):
+    pick_f, pick_r, _, _ = orders(mp[0], n_mp, w_x.shape[0])
+    w = jnp.concatenate([w_x[...], w_bc[:, 0:NSTATE]], axis=1)
+    o_f[...] = jnp.dot(pick_f, w, preferred_element_type=f32).astype(bf16)
+    o_r[...] = jnp.dot(pick_r, w, preferred_element_type=f32).astype(bf16)
+    rows = [
+        lax.dot_general(w_dt[...], pick, (((1,), (1,)), ((), ())), preferred_element_type=f32)
+        for pick in (pick_f, pick_r)
+    ]
+    o_dt[...] = jnp.concatenate(rows, axis=0).astype(bf16)
+
+
+def prepare_2_body(n_mp, mp, w_bc, w_z, w_out, o_f, o_r, p_f, p_r):
+    pick_f, pick_r, out_f, out_r = orders(mp[0], n_mp, w_z.shape[0])
+    w = jnp.concatenate([w_bc[:, NSTATE:], w_z[...]], axis=1)
+    o_f[...] = jnp.dot(pick_f, w, preferred_element_type=f32).astype(bf16)
+    o_r[...] = jnp.dot(pick_r, w, preferred_element_type=f32).astype(bf16)
+    p_f[...] = jnp.dot(w_out[...], out_f, preferred_element_type=f32).astype(bf16)
+    p_r[...] = jnp.dot(w_out[...], out_r, preferred_element_type=f32).astype(bf16)
+
+
+def prepare(body, name, n_mp, mp, arrays, shapes):
+    return pl.pallas_call(
+        functools.partial(body, n_mp),
+        grid=(1,),
+        in_specs=[SMEM] + [whole(a.shape) for a in arrays],
+        out_specs=[whole(a) for a in shapes],
+        out_shape=[jax.ShapeDtypeStruct(a, bf16) for a in shapes],
+        compiler_params=params(20),
+        cost_estimate=cost(1e9, 3e6),
+        name=name,
+    )(mp, *arrays)
 
 
 def row_spread():
@@ -665,28 +754,18 @@
     low = lax.ppermute(hidden[rows - EDGE :], "ctx", [(i, i + 1) for i in range(n_ctx - 1)])
     high = lax.ppermute(hidden[:EDGE], "ctx", [(i + 1, i) for i in range(n_ctx - 1)])
     outer = jnp.concatenate([low, hidden[: run + EDGE], hidden[3 * run - EDGE :], high], axis=0)
+
+    width = w_x.shape[0]
+    place, outer = lax.optimization_barrier((mp[None].astype(jnp.int32), outer))
     hs_1 = [outer] + [around(outer, "mp", n_mp, s) for s in range(1, n_mp)]
-
-    width = w_x.shape[0]
-    here = width // n_mp
-    at = jnp.arange(width, dtype=jnp.int32)
-    place = ((mp - at // here) % n_mp) * here + at % here
-    pick_f = (place[:, None] == at[None, :]).astype(bf16)
-    pick_r = (width - 1 - place[:, None] == at[None, :]).astype(bf16)
-    w_1 = jnp.concatenate([w_x, w_bc[:, :NSTATE]], axis=1)
-    w_2 = jnp.concatenate([w_bc[:, NSTATE:], w_z], axis=1)
-    w_1f, w_1r, w_2f, w_2r = (
-        jnp.dot(pick, w, preferred_element_type=f32).astype(bf16)
-        for w in (w_1, w_2) for pick in (pick_f, pick_r)
+    w_1f, w_1r, wdt = prepare(
+        prepare_1_body, "prepare_1", n_mp, place, (w_x, w_bc, w_dt.T),
+        [(width, MIX), (width, MIX), (8, width)],
     )
-    wdt = jnp.concatenate(
-        [jnp.dot(pick, w_dt, preferred_element_type=f32).astype(bf16).T for pick in (pick_f, pick_r)], axis=0
+    w_2f, w_2r, w_of, w_or = prepare(
+        prepare_2_body, "prepare_2", n_mp, place, (w_bc, w_z, w_out),
+        [(width, MIX), (width, MIX), w_out.shape, w_out.shape],
     )
-    goal = ((mp + at // here) % n_mp) * here + at % here
-    out_pick_f = (goal[None, :] == at[:, None]).astype(bf16)
-    out_pick_r = (width - 1 - goal[None, :] == at[:, None]).astype(bf16)
-    w_of = jnp.dot(w_out, out_pick_f, preferred_element_type=f32).astype(bf16)
-    w_or = jnp.dot(w_out, out_pick_r, preferred_element_type=f32).astype(bf16)
 
     gain = norm_gain[None, :]
     spread = jnp.asarray(head_spread(), bf16)
@@ -698,38 +777,41 @@
     weights_2 = (w_2f, w_2r, conv_x, conv_bc)
 
     xb_f, xb_r, cum, dt, fs_0, *middle_states = local_states(0, *first, hs_0, *weights_1)
-    locals_0 = intra(
-        0, 0, 1, piece_lengths, meta, skip_gain, hs_0, *weights_2, xb_f, xb_r, cum, dt, ()
-    )
-    hs_1, locals_0 = lax.optimization_barrier((tuple(hs_1), tuple(locals_0)))
+    arguments = [(piece_lengths, meta, skip_gain, hs_0, *weights_2, xb_f, xb_r, cum, dt)]
+    done = [(), ()]
+
+    def beside(chunk, part, received):
+        new = intra(chunk, part, INTRA_PARTS, *arguments[chunk], done[chunk])
+        received, new = lax.optimization_barrier((received, tuple(new)))
+        done[chunk] = new
+        return received
+
+    hs_1 = beside(0, 0, tuple(hs_1))
     xb_f, xb_r, cum, dt, fs_1, starts, decays, *pays = local_states(
         1, *first, hs_1, *weights_1, middle_states
     )
-    locals_1 = ()
-
-    def beside(part, received):
-        nonlocal locals_1
-        locals_1 = intra(
-            1, part, INTRA_PARTS, piece_lengths, meta, skip_gain, hs_1, *weights_2, xb_f, xb_r, cum, dt, locals_1
-        )
-        received, locals_1 = lax.optimization_barrier((received, tuple(locals_1)))
-        return received
+    arguments.append((piece_lengths, meta, skip_gain, hs_1, *weights_2, xb_f, xb_r, cum, dt))
 
     def moved(arrays, stride):
         return [lax.ppermute(a, "ctx", digit_perm(n_ctx, stride, s)) for s, a in zip((1, 2, 3), arrays)]
 
-    pre_s, pre_a, pay = join_group(meta, [pays[0]] + beside(0, moved(pays[1:], 1)))
-    low_s, low_a, top = join_middle(meta, [pay] + beside(1, moved([pay] * 3, 4)))
-    back = join_top(meta, moved([top] * 3, 16) + [low_s, low_a, pre_s, pre_a])
+    pre_s, pre_a, pay = join_group(meta, [pays[0]] + beside(0, 1, moved(pays[1:], 1)))
+    low_s, low_a, top = join_middle(meta, [pay] + beside(1, 0, moved([pay] * 3, 4)))
+    back = join_top(meta, beside(1, 1, moved([top] * 3, 16)) + [low_s, low_a, pre_s, pre_a])
     quarters = [back[0]] + moved(back[1:], 1)
 
-    gated = gate(0, meta, locals_0, fs_0, starts, decays, quarters, gain, spread, ())
-    g_f, g_r, sums = gate(1, meta, locals_1, fs_1, starts, decays, quarters, gain, spread, gated)
+    gated = gate(0, meta, done[0], fs_0, starts, decays, quarters, gain, spread, ())
+    g_f, g_r, sums = gate(1, meta, done[1], fs_1, starts, decays, quarters, gain, spread, gated)
     all_sums = [sums] + [around(sums, "mp", n_mp, s) for s in range(1, n_mp)]
-    total, *sent = project_out(g_f, g_r, all_sums, w_of, w_or, spread_rows)
-    for s, piece in enumerate(sent):
-        total = total + around(piece, "mp", n_mp, s + 1).astype(f32)
-    return total.astype(bf16)
+    tail = (g_f, g_r, all_sums, w_of, w_or, spread_rows)
+    own_a, up_a, far_a, down_a = project_out(0, (f32, f32, bf16, bf16), *tail)
+    far_a = around(far_a, "mp", n_mp, 1)
+    own_b, up_b, far_b, down_b = project_out(1, (f32, bf16, bf16, f32), *tail)
+    far_b = around(far_b, "mp", n_mp, n_mp - 1)
+    down_a, up_b = around(down_a, "mp", n_mp, n_mp - 1), around(up_b, "mp", n_mp, 1)
+    up_a, down_b = join_shares(up_a, far_a, down_b, far_b)
+    up_a, down_b = around(up_a, "mp", n_mp, 1), around(down_b, "mp", n_mp, n_mp - 1)
+    return last_sum(own_a, down_a, up_a, own_b, up_b, down_b)
 
 
 def solution(mesh):

time: 120 us -> 123 us (1.025)
  starting transfers between devices: 37.2 us -> 53.5 us
  waiting for transfers between devices: 37.9 us -> 24 us
  matrix products: 5.74 us -> 0 us
  Pallas kernels: 33.7 us -> 37.2 us
  local copies, waits for them, and re-layouts: 2.83 us -> 5.33 us
    ppermute x12 -> x15, waiting for transfers between devices: 33.4 us -> 15.5 us  [around(): lax.ppermute(array, axis, [(i, (i + shift) % count) for i in range(count)])]
    ppermute x12 -> x15, starting transfers between devices: 12.3 us -> 21.4 us  [around(): lax.ppermute(array, axis, [(i, (i + shift) % count) for i in range(count)])]
    ppermute x12, starting transfers between devices: 22.3 us -> 29.5 us  [moved(): lax.ppermute(a, 'ctx', digit_perm(n_ctx, stride, s))]
    dot_general x8 -> x0, matrix products: 5.74 us -> none  [the longest x4 2.88 us: shards(): jnp.dot(pick, w, preferred_element_type=f32).astype(bf16)]
    pallas_call x1 -> x6, Pallas kernels: 3.24 us -> 6.2 us  [the longest x2 3.25 us: project_out(): pl.pallas_call(k4_body, grid=(HERE,), in_specs=[g_in, g_in] + [s_in] * 4...]
    ppermute x1, waiting for transfers between devices: 0.01 us -> 2.75 us  [shards(): lax.ppermute(hidden[:EDGE], 'ctx', [(i + 1, i) for i in range(n_ctx - 1)])]
    unnamed x26 -> x28, local copies, waits for them, and re-layouts: 0.08 us -> 2.66 us
    pallas_call x3 -> x4, Pallas kernels: 11.9 us -> 12.4 us  [intra(): pl.pallas_call(functools.partial(k2_body, chunk, base, len(before)), grid...]
  transfers between devices with their start and end apart: 26 -> 29, of which waited for: 13 -> 16; matrix products, arithmetic and copies ran while one was open for 6% -> 1% of each run, Pallas kernels for 15% -> 18%
where the time goes in v1:
time: 123 us; the launch traced here: 121 us
  starting transfers between devices  53.5 us (43%)
  Pallas kernels  37.2 us (30%)
  waiting for transfers between devices  24 us (20%)
  local copies, waits for them, and re-layouts  5.33 us (4%)
    ppermute x12, starting transfers between devices, moved(): lax.ppermute(a, 'ctx', digit_perm(n_ctx, stride, s))  29.5 us
    ppermute x15, starting transfers between devices, around(): lax.ppermute(array, axis, [(i, (i + shift) % count) for i in range(count)])  21.4 us
    ppermute x15, waiting for transfers between devices, around(): lax.ppermute(array, axis, [(i, (i + shift) % count) for i in range(count)])  15.5 us
    pallas_call x4, Pallas kernels, intra(): pl.pallas_call(functools.partial(k2_body, chunk, base, len(before)), grid...  12.4 us
    pallas_call x2, Pallas kernels, local_states(): pl.pallas_call(functools.partial(k1_body, chunk), grid=(HERE,), in_specs=...  11.2 us
    ppermute x12, waiting for transfers between devices, moved(): lax.ppermute(a, 'ctx', digit_perm(n_ctx, stride, s))  5.75 us
    pallas_call x2, Pallas kernels, gate(): pl.pallas_call(k3_body, grid=(HERE,), in_specs=[SMEM, c_in, c_in, y_in, y...  5.6 us
    pallas_call x2, Pallas kernels, project_out(): pl.pallas_call(k4_body, grid=(HERE,), in_specs=[g_in, g_in] + [s_in] * 4...  3.25 us
  transfers between devices with their start and end apart: 29, of which 16 were waited for; matrix products, arithmetic and copies ran while one was open for 1% of the time, Pallas kernels for 18%

profile of v1, /device:TPU:24, one launch (start us, length us, event | category | flops | bytes accessed | tf_op | source)
XLA Modules:
  0.0 120.9 jit_solution(6793181366281890515)
XLA Ops:
  1.8 2.7 %collective-permute-start.6 = (bf16[1056,128]{1,0:T(8,128)(2,1)S(1)}, bf16[1056,128]{1,0:T(8,128)(2,1)S(1)}, u32[]{:S(2)}, u32[]{:S(2)}) collective-permute-start(bf16[1056,128]{1,0:T(8,128)(2,1)S(1)} %slice.19.h0), channel_id=1, source_target_pairs={{0,2},{1,3},{2,0},{3,1},{4,6},{5,7},{6,4},{7,5},{8,10},{9,11},{10,... | collective-permute-start | bytes 811016 | tf_op jit(solution)/shard_map/ppermute | solution.py:729
  9.4 2.7 %collective-permute-done.1 = bf16[16,128]{1,0:T(8,128)(2,1)S(1)} collective-permute-done((bf16[16,128]{1,0:T(8,128)(2,1)S(1)}, bf16[16,128]{1,0:T(8,128)(2,1)S(1)}, u32[]{:S(2)}, u32[]{:S(2)}) %collective-permute-start.1) | collective-permute-done | bytes 4128 | tf_op jit(solution)/shard_map/ppermute | solution.py:755
  12.5 2.2 %collective-permute-start.3 = (bf16[1088,128]{1,0:T(8,128)(2,1)S(1)}, bf16[1088,128]{1,0:T(8,128)(2,1)S(1)}, u32[]{:S(2)}, u32[]{:S(2)}) collective-permute-start(bf16[1088,128]{1,0:T(8,128)(2,1)S(1)} %pad_maximum_fusion.h0), channel_id=1, source_target_pairs={{0,2},{1,3},{2,0},{3,1},{4,6},{5,7},{6,4},{7,5},{8,10},{9,11},{10,... | collective-permute-start | bytes 835592 | tf_op jit(solution)/shard_map/ppermute | solution.py:729
  19.3 2.9 %collective-permute-start.2 = (bf16[1088,128]{1,0:T(8,128)(2,1)S(1)}, bf16[1088,128]{1,0:T(8,128)(2,1)S(1)}, u32[]{:S(2)}, u32[]{:S(2)}) collective-permute-start(bf16[1088,128]{1,0:T(8,128)(2,1)S(1)} %pad_maximum_fusion.h0), channel_id=1, source_target_pairs={{0,1},{1,2},{2,3},{3,0},{4,5},{5,6},{6,7},{7,4},{8,9},{9,10},{10,1... | collective-permute-start | bytes 835592 | tf_op jit(solution)/shard_map/ppermute | solution.py:729
  22.3 5.5 %local_states.2 = (bf16[1024,384]{1,0:T(8,128)(2,1)S(1)}, bf16[1024,384]{1,0:T(8,128)(2,1)S(1)}, f32[8,1024]{1,0:T(8,128)S(1)}, f32[8,1024]{1,0:T(8,128)S(1)}, f...) custom-call(s32[16]{0:T(128)S(1)} %copy-done.11, s32[4]{0:T(128)S(1)} %pad_add_fusion.meta, ...), custom_call_target="tpu_custom_call" | custom-call | flops 6144000000 | bytes 4096000 | tf_op jit(solution)/shard_map/local_states/pallas_call | solution.py:309
  27.8 3.1 %intra.4 = (bf16[1024,128]{1,0:T(8,128)(2,1)S(1)}, bf16[1024,128]{1,0:T(8,128)(2,1)S(1)}, f32[1024,256]{1,0:T(8,128)S(1)}, f32[1024,256]{1,0:T(8,128)S(1)}, f32[...) custom-call(s32[16]{0:T(128)S(1)} %copy-done.11, s32[4]{0:T(128)S(1)} %pad_add_fusion.meta, f32[4]{0:T(128)S(1)} %copy-done.12, ...), custom_call_target="tpu_custom_call" | custom-call | flops 2560000000 | bytes 2560000 | tf_op jit(solution)/shard_map/intra/pallas_call | solution.py:406
  31.0 5.7 %local_states.3 = (bf16[1024,384]{1,0:T(8,128)(2,1)S(1)}, bf16[1024,384]{1,0:T(8,128)(2,1)S(1)}, f32[8,1024]{1,0:T(8,128)S(1)}, f32[8,1024]{1,0:T(8,128)S(1)}, f...) custom-call(s32[16]{0:T(128)S(1)} %copy-done.11, ...), custom_call_target="tpu_custom_call" | custom-call | flops 6144000000 | bytes 4096000 | tf_op jit(solution)/shard_map/local_states/pallas_call | solution.py:309
  36.7 2.1 %collective-permute-start.8 = (bf16[80,256]{1,0:T(8,128)(2,1)S(1)}, bf16[80,256]{1,0:T(8,128)(2,1)S(1)}, u32[]{:S(2)}, u32[]{:S(2)}) collective-permute-start(bf16[80,256]{1,0:T(8,128)(2,1)S(1)} %get-tuple-element.143), channel_id=1, source_target_pairs={{0,4},{4,8},{8,12},{12,0},{16,20},{20,24},{24,28},{28,16},{32,36},... | collective-permute-start | bytes 122888 | tf_op jit(solution)/shard_map/ppermute | solution.py:796
  38.8 1.7 %collective-permute-start.9 = (bf16[80,256]{1,0:T(8,128)(2,1)S(1)}, bf16[80,256]{1,0:T(8,128)(2,1)S(1)}, u32[]{:S(2)}, u32[]{:S(2)}) collective-permute-start(bf16[80,256]{1,0:T(8,128)(2,1)S(1)} %get-tuple-element.144), channel_id=1, source_target_pairs={{0,8},{4,12},{8,0},{12,4},{16,24},{20,28},{24,16},{28,20},{32,40},... | collective-permute-start | bytes 122888 | tf_op jit(solution)/shard_map/ppermute | solution.py:796
  40.6 3.1 %intra.5 = (bf16[1024,128]{1,0:T(8,128)(2,1)S(1)}, bf16[1024,128]{1,0:T(8,128)(2,1)S(1)}, f32[1024,256]{1,0:T(8,128)S(1)}, f32[1024,256]{1,0:T(8,128)S(1)}, f32[...) custom-call(s32[16]{0:T(128)S(1)} %copy-done.11, ...), custom_call_target="tpu_custom_call", output_to_operand_aliasing={{0}: (15, {}), {1}: (16, {}), {2}: (17, {}), {3}: (18, {}),... | custom-call | flops 2560000000 | bytes 2560000 | tf_op jit(solution)/shard_map/intra/pallas_call | solution.py:406
  44.3 5.4 %collective-permute-start.13 = (bf16[80,256]{1,0:T(8,128)(2,1)S(1)}, bf16[80,256]{1,0:T(8,128)(2,1)S(1)}, u32[]{:S(2)}, u32[]{:S(2)}) collective-permute-start(bf16[80,256]{1,0:T(8,128)(2,1)S(1)} %get-tuple-element.161.own), channel_id=1, source_target_pairs={{0,48},{4,52},{8,56},{12,60},{16,0},{20,4},{24,8},{28,12},{32,16},... | collective-permute-start | bytes 122888 | tf_op jit(solution)/shard_map/ppermute | solution.py:796
  49.7 12.5 %collective-permute-start.12 = (bf16[80,256]{1,0:T(8,128)(2,1)S(1)}, bf16[80,256]{1,0:T(8,128)(2,1)S(1)}, u32[]{:S(2)}, u32[]{:S(2)}) collective-permute-start(bf16[80,256]{1,0:T(8,128)(2,1)S(1)} %get-tuple-element.161.own), channel_id=1, source_target_pairs={{0,32},{4,36},{8,40},{12,44},{16,48},{20,52},{24,56},{28,60},{32,0... | collective-permute-start | bytes 122888 | tf_op jit(solution)/shard_map/ppermute | solution.py:796
  62.7 3.1 %intra.6 = (bf16[1024,128]{1,0:T(8,128)(2,1)S(1)}, bf16[1024,128]{1,0:T(8,128)(2,1)S(1)}, f32[1024,256]{1,0:T(8,128)S(1)}, f32[1024,256]{1,0:T(8,128)S(1)}, f32[...) custom-call(s32[16]{0:T(128)S(1)} %copy-done.11, s32[4]{0:T(128)S(1)} %pad_add_fusion.meta, f32[4]{0:T(128)S(1)} %copy-done.12, ...), custom_call_target="tpu_custom_call" | custom-call | flops 2560000000 | bytes 2560000 | tf_op jit(solution)/shard_map/intra/pallas_call | solution.py:406
  65.8 1.4 %collective-permute-done.12.r2 = bf16[80,256]{1,0:T(8,128)(2,1)S(1)} collective-permute-done((bf16[80,256]{1,0:T(8,128)(2,1)S(1)}, bf16[80,256]{1,0:T(8,128)(2,1)S(1)}, u32[]{:S(2)}, u32[]{:S(2)}) %collective-permute-start.12) | collective-permute-done | bytes 40992 | tf_op jit(solution)/shard_map/ppermute | solution.py:796
  69.2 2.7 %collective-permute-start.16 = (bf16[80,256]{1,0:T(8,128)(2,1)S(1)}, bf16[80,256]{1,0:T(8,128)(2,1)S(1)}, u32[]{:S(2)}, u32[]{:S(2)}) collective-permute-start(bf16[80,256]{1,0:T(8,128)(2,1)S(1)} %get-tuple-element.175), channel_id=1, source_target_pairs={{0,192},{4,196},{8,200},{12,204},{16,208},{20,212},{24,216},{28,22... | collective-permute-start | bytes 122888 | tf_op jit(solution)/shard_map/ppermute | solution.py:796
  73.4 3.1 %intra.7 = (bf16[1024,128]{1,0:T(8,128)(2,1)S(1)}, bf16[1024,128]{1,0:T(8,128)(2,1)S(1)}, f32[1024,256]{1,0:T(8,128)S(1)}, f32[1024,256]{1,0:T(8,128)S(1)}, f32[...) custom-call(s32[16]{0:T(128)S(1)} %copy-done.11, ...), custom_call_target="tpu_custom_call", output_to_operand_aliasing={{0}: (15, {}), {1}: (16, {}), {2}: (17, {}), {3}: (18, {}),... | custom-call | flops 2560000000 | bytes 2560000 | tf_op jit(solution)/shard_map/intra/pallas_call | solution.py:406
  78.6 1.6 %collective-permute-start.18 = (bf16[64,256]{1,0:T(8,128)(2,1)S(1)}, bf16[64,256]{1,0:T(8,128)(2,1)S(1)}, u32[]{:S(2)}, u32[]{:S(2)}) collective-permute-start(bf16[64,256]{1,0:T(8,128)(2,1)S(1)} %get-tuple-element.206), channel_id=1, source_target_pairs={{0,8},{4,12},{8,0},{12,4},{16,24},{20,28},{24,16},{28,20},{32,40},... | collective-permute-start | bytes 98312 | tf_op jit(solution)/shard_map/ppermute | solution.py:796
  83.2 2.8 %gate.2 = (bf16[2048,256]{1,0:T(8,128)(2,1)S(1)}, bf16[2048,256]{1,0:T(8,128)(2,1)S(1)}, f32[2,2048]{1,0:T(2,128)S(1)}) custom-call(s32[4]{0:T(128)S(1)} %pad_add_fusion.meta, bf16[1024,128]{1,0:T(8,128)(2,1)S(1)} %get-tuple-element.208.c_f, bf16[1024,128]{1,0:T(8,128)(2,1)S(1)} %get-tuple-element.209.c_r, f32[1024,256]{1,0:T(8,128)S(1)} %get-tuple-element.210.y_f, ...), custom_call_target="tpu_custom_call" | custom-call | flops 614400000 | bytes 6144000 | tf_op jit(solution)/shard_map/gate/pallas_call | solution.py:576
  85.9 2.8 %gate.3 = (bf16[2048,256]{1,0:T(8,128)(2,1)S(1)}, bf16[2048,256]{1,0:T(8,128)(2,1)S(1)}, f32[2,2048]{1,0:T(2,128)S(1)}) custom-call(s32[4]{0:T(128)S(1)} %pad_add_fusion.meta, bf16[1024,128]{1,0:T(8,128)(2,1)S(1)} %get-tuple-element.188.c_f, ...), custom_call_target="tpu_custom_call", output_to_operand_aliasing={{0}: (16, {}), {1}: (17, {}), {2}: (18, {})} | custom-call | flops 614400000 | bytes 6144000 | tf_op jit(solution)/shard_map/gate/pallas_call | solution.py:576
  88.9 1.9 %collective-permute-start.21 = (f32[2,2048]{1,0:T(2,128)S(1)}, f32[2,2048]{1,0:T(2,128)S(1)}, u32[]{:S(2)}, u32[]{:S(2)}) collective-permute-start(f32[2,2048]{1,0:T(2,128)S(1)} %get-tuple-element.220.s0), channel_id=1, source_target_pairs={{0,2},{1,3},{2,0},{3,1},{4,6},{5,7},{6,4},{7,5},{8,10},{9,11},{10,... | collective-permute-start | bytes 49160 | tf_op jit(solution)/shard_map/ppermute | solution.py:729
  90.8 2.0 %collective-permute-start.20 = (f32[2,2048]{1,0:T(2,128)S(1)}, f32[2,2048]{1,0:T(2,128)S(1)}, u32[]{:S(2)}, u32[]{:S(2)}) collective-permute-start(f32[2,2048]{1,0:T(2,128)S(1)} %get-tuple-element.220.s0), channel_id=1, source_target_pairs={{0,1},{1,2},{2,3},{3,0},{4,5},{5,6},{6,7},{7,4},{8,9},{9,10},{10,1... | collective-permute-start | bytes 49160 | tf_op jit(solution)/shard_map/ppermute | solution.py:729
  94.9 1.6 %project_out.3 = (f32[1024,128]{1,0:T(8,128)S(1)}, bf16[1024,128]{1,0:T(8,128)(2,1)S(1)}, bf16[1024,128]{1,0:T(8,128)(2,1)S(1)}, f32[1024,128]{1,0:T(8,128)S(1)}) custom-call(bf16[2048,256]{1,0:T(8,128)(2,1)S(1)} %get-tuple-element.218.g_f, bf16[2048,256]{1,0:T(8,128)(2,1)S(1)} %get-tuple-element.219.g_r, f32[2,2048]{1,0:T(2,128)S(1)} %get-tuple-element.220.s0, ...), custom_call_target="tpu_custom_call" | custom-call | flops 1024000000 | bytes 3072000 | tf_op jit(solution)/shard_map/project_out/pallas_call | solution.py:620
  96.5 1.9 %collective-permute-start.25 = (bf16[1024,128]{1,0:T(8,128)(2,1)S(1)}, bf16[1024,128]{1,0:T(8,128)(2,1)S(1)}, u32[]{:S(2)}, u32[]{:S(2)}) collective-permute-start(bf16[1024,128]{1,0:T(8,128)(2,1)S(1)} %get-tuple-element.228), channel_id=1, source_target_pairs={{0,3},{1,0},{2,1},{3,2},{4,7},{5,4},{6,5},{7,6},{8,11},{9,8},{10,9... | collective-permute-start | bytes 786440 | tf_op jit(solution)/shard_map/ppermute | solution.py:729
  98.4 1.6 %project_out.2 = (f32[1024,128]{1,0:T(8,128)S(1)}, f32[1024,128]{1,0:T(8,128)S(1)}, bf16[1024,128]{1,0:T(8,128)(2,1)S(1)}, bf16[1024,128]{1,0:T(8,128)(2,1)S(1)}) custom-call(bf16[2048,256]{1,0:T(8,128)(2,1)S(1)} %get-tuple-element.218.g_f, bf16[2048,256]{1,0:T(8,128)(2,1)S(1)} %get-tuple-element.219.g_r, f32[2,2048]{1,0:T(2,128)S(1)} %get-tuple-element.220.s0, ...), custom_call_target="tpu_custom_call" | custom-call | flops 1024000000 | bytes 3072000 | tf_op jit(solution)/shard_map/project_out/pallas_call | solution.py:620
  100.1 1.5 %collective-permute-start.24 = (bf16[1024,128]{1,0:T(8,128)(2,1)S(1)}, bf16[1024,128]{1,0:T(8,128)(2,1)S(1)}, u32[]{:S(2)}, u32[]{:S(2)}) collective-permute-start(bf16[1024,128]{1,0:T(8,128)(2,1)S(1)} %get-tuple-element.226), channel_id=1, source_target_pairs={{0,1},{1,2},{2,3},{3,0},{4,5},{5,6},{6,7},{7,4},{8,9},{9,10},{10,1... | collective-permute-start | bytes 786440 | tf_op jit(solution)/shard_map/ppermute | solution.py:729
  101.5 1.6 %collective-permute-start.27 = (bf16[1024,128]{1,0:T(8,128)(2,1)S(1)}, bf16[1024,128]{1,0:T(8,128)(2,1)S(1)}, u32[]{:S(2)}, u32[]{:S(2)}) collective-permute-start(bf16[1024,128]{1,0:T(8,128)(2,1)S(1)} %get-tuple-element.231), channel_id=1, source_target_pairs={{0,1},{1,2},{2,3},{3,0},{4,5},{5,6},{6,7},{7,4},{8,9},{9,10},{10,1... | collective-permute-start | bytes 786440 | tf_op jit(solution)/shard_map/ppermute | solution.py:729
  103.5 2.2 %collective-permute-done.25.b2 = bf16[1024,128]{1,0:T(8,128)(2,1)S(1)} collective-permute-done((bf16[1024,128]{1,0:T(8,128)(2,1)S(1)}, bf16[1024,128]{1,0:T(8,128)(2,1)S(1)}, u32[]{:S(2)}, u32[]{:S(2)}) %collective-permute-start.25) | collective-permute-done | bytes 262176 | tf_op jit(solution)/shard_map/ppermute | solution.py:729
  105.7 3.7 %collective-permute-done.24.b1 = bf16[1024,128]{1,0:T(8,128)(2,1)S(1)} collective-permute-done((bf16[1024,128]{1,0:T(8,128)(2,1)S(1)}, bf16[1024,128]{1,0:T(8,128)(2,1)S(1)}, u32[]{:S(2)}, u32[]{:S(2)}) %collective-permute-start.24) | collective-permute-done | bytes 262176 | tf_op jit(solution)/shard_map/ppermute | solution.py:729
  109.5 2.7 %collective-permute-start.26 = (bf16[1024,128]{1,0:T(8,128)(2,1)S(1)}, bf16[1024,128]{1,0:T(8,128)(2,1)S(1)}, u32[]{:S(2)}, u32[]{:S(2)}) collective-permute-start(bf16[1024,128]{1,0:T(8,128)(2,1)S(1)} %get-tuple-element.229), channel_id=1, source_target_pairs={{0,1},{1,2},{2,3},{3,0},{4,5},{5,6},{6,7},{7,4},{8,9},{9,10},{10,1... | collective-permute-start | bytes 786440 | tf_op jit(solution)/shard_map/ppermute | solution.py:729
  112.2 2.8 %collective-permute-done.27.b1 = bf16[1024,128]{1,0:T(8,128)(2,1)S(1)} collective-permute-done((bf16[1024,128]{1,0:T(8,128)(2,1)S(1)}, bf16[1024,128]{1,0:T(8,128)(2,1)S(1)}, u32[]{:S(2)}, u32[]{:S(2)}) %collective-permute-start.27) | collective-permute-done | bytes 262176 | tf_op jit(solution)/shard_map/ppermute | solution.py:729
  115.0 3.2 %collective-permute-done.26.a2 = bf16[1024,128]{1,0:T(8,128)(2,1)S(1)} collective-permute-done((bf16[1024,128]{1,0:T(8,128)(2,1)S(1)}, bf16[1024,128]{1,0:T(8,128)(2,1)S(1)}, u32[]{:S(2)}, u32[]{:S(2)}) %collective-permute-start.26) | collective-permute-done | bytes 262176 | tf_op jit(solution)/shard_map/ppermute | solution.py:729
  118.2 1.6 %collective-permute-done.28.b2 = bf16[1024,128]{1,0:T(8,128)(2,1)S(1)} collective-permute-done((bf16[1024,128]{1,0:T(8,128)(2,1)S(1)}, bf16[1024,128]{1,0:T(8,128)(2,1)S(1)}, u32[]{:S(2)}, u32[]{:S(2)}) %collective-permute-start.28) | collective-permute-done | bytes 262176 | tf_op jit(solution)/shard_map/ppermute | solution.py:729
  (76 shorter events, 24.6 us)
Async XLA Ops:
  1.0 18.3 %collective-permute-start.7 = (bf16[1056,128]{1,0:T(8,128)(2,1)S(1)}, bf16[1056,128]{1,0:T(8,128)(2,1)S(1)}, u32[]{:S(2)}, u32[]{:S(2)}) collective-permute-start(bf16[1056,128]{1,0:T(8,128)(2,1)S(1)} %slice.19.h0), channel_id=1, source_target_pairs={{0,3},{1,0},{2,1},{3,2},{4,7},{5,4},{6,5},{7,6},{8,11},{9,8},{10,9... | collective-permute-start | bytes 811016 | tf_op jit(solution)/shard_map/ppermute | solution.py:729
  1.8 20.5 %collective-permute-start.6 = (bf16[1056,128]{1,0:T(8,128)(2,1)S(1)}, bf16[1056,128]{1,0:T(8,128)(2,1)S(1)}, u32[]{:S(2)}, u32[]{:S(2)}) collective-permute-start(bf16[1056,128]{1,0:T(8,128)(2,1)S(1)} %slice.19.h0), channel_id=1, source_target_pairs={{0,2},{1,3},{2,0},{3,1},{4,6},{5,7},{6,4},{7,5},{8,10},{9,11},{10,... | collective-permute-start | bytes 811016 | tf_op jit(solution)/shard_map/ppermute | solution.py:729
  4.5 17.8 %collective-permute-start.5 = (bf16[1056,128]{1,0:T(8,128)(2,1)S(1)}, bf16[1056,128]{1,0:T(8,128)(2,1)S(1)}, u32[]{:S(2)}, u32[]{:S(2)}) collective-permute-start(bf16[1056,128]{1,0:T(8,128)(2,1)S(1)} %slice.19.h0), channel_id=1, source_target_pairs={{0,1},{1,2},{2,3},{3,0},{4,5},{5,6},{6,7},{7,4},{8,9},{9,10},{10,1... | collective-permute-start | bytes 811016 | tf_op jit(solution)/shard_map/ppermute | solution.py:729
  5.6 3.8 %collective-permute-start = (bf16[16,128]{1,0:T(8,128)(2,1)S(1)}, bf16[16,128]{1,0:T(8,128)(2,1)S(1)}, u32[]{:S(2)}, u32[]{:S(2)}) collective-permute-start(bf16[16,128]{1,0:T(8,128)(2,1)S(1)} %get-tuple-element.233), channel_id=1, source_target_pairs={{0,4},{4,8},{8,12},{12,16},{16,20},{20,24},{24,28},{28,32},{32,36}... | collective-permute-start | bytes 12296 | tf_op jit(solution)/shard_map/ppermute | solution.py:754
  6.9 5.2 %collective-permute-start.1 = (bf16[16,128]{1,0:T(8,128)(2,1)S(1)}, bf16[16,128]{1,0:T(8,128)(2,1)S(1)}, u32[]{:S(2)}, u32[]{:S(2)}) collective-permute-start(bf16[16,128]{1,0:T(8,128)(2,1)S(1)} %get-tuple-element.234), channel_id=1, source_target_pairs={{4,0},{8,4},{12,8},{16,12},{20,16},{24,20},{28,24},{32,28},{36,32}... | collective-permute-start | bytes 12296 | tf_op jit(solution)/shard_map/ppermute | solution.py:755
  12.1 6.1 %copy-start.5 = (bf16[256,512]{1,0:T(8,128)(2,1)S(1)}, bf16[256,512]{1,0:T(8,128)(2,1)}, u32[]{:S(2)}) copy-start(bf16[256,512]{1,0:T(8,128)(2,1)} %w_out.1) | copy-start | bytes 786436
  12.2 18.8 %collective-permute-start.4 = (bf16[1088,128]{1,0:T(8,128)(2,1)S(1)}, bf16[1088,128]{1,0:T(8,128)(2,1)S(1)}, u32[]{:S(2)}, u32[]{:S(2)}) collective-permute-start(bf16[1088,128]{1,0:T(8,128)(2,1)S(1)} %pad_maximum_fusion.h0), channel_id=1, source_target_pairs={{0,3},{1,0},{2,1},{3,2},{4,7},{5,4},{6,5},{7,6},{8,11},{9,8},{10,9... | collective-permute-start | bytes 835592 | tf_op jit(solution)/shard_map/ppermute | solution.py:729
  12.5 18.5 %collective-permute-start.3 = (bf16[1088,128]{1,0:T(8,128)(2,1)S(1)}, bf16[1088,128]{1,0:T(8,128)(2,1)S(1)}, u32[]{:S(2)}, u32[]{:S(2)}) collective-permute-start(bf16[1088,128]{1,0:T(8,128)(2,1)S(1)} %pad_maximum_fusion.h0), channel_id=1, source_target_pairs={{0,2},{1,3},{2,0},{3,1},{4,6},{5,7},{6,4},{7,5},{8,10},{9,11},{10,... | collective-permute-start | bytes 835592 | tf_op jit(solution)/shard_map/ppermute | solution.py:729
  19.3 11.6 %collective-permute-start.2 = (bf16[1088,128]{1,0:T(8,128)(2,1)S(1)}, bf16[1088,128]{1,0:T(8,128)(2,1)S(1)}, u32[]{:S(2)}, u32[]{:S(2)}) collective-permute-start(bf16[1088,128]{1,0:T(8,128)(2,1)S(1)} %pad_maximum_fusion.h0), channel_id=1, source_target_pairs={{0,1},{1,2},{2,3},{3,0},{4,5},{5,6},{6,7},{7,4},{8,9},{9,10},{10,1... | collective-permute-start | bytes 835592 | tf_op jit(solution)/shard_map/ppermute | solution.py:729
  36.7 7.0 %collective-permute-start.8 = (bf16[80,256]{1,0:T(8,128)(2,1)S(1)}, bf16[80,256]{1,0:T(8,128)(2,1)S(1)}, u32[]{:S(2)}, u32[]{:S(2)}) collective-permute-start(bf16[80,256]{1,0:T(8,128)(2,1)S(1)} %get-tuple-element.143), channel_id=1, source_target_pairs={{0,4},{4,8},{8,12},{12,0},{16,20},{20,24},{24,28},{28,16},{32,36},... | collective-permute-start | bytes 122888 | tf_op jit(solution)/shard_map/ppermute | solution.py:796
  38.8 4.9 %collective-permute-start.9 = (bf16[80,256]{1,0:T(8,128)(2,1)S(1)}, bf16[80,256]{1,0:T(8,128)(2,1)S(1)}, u32[]{:S(2)}, u32[]{:S(2)}) collective-permute-start(bf16[80,256]{1,0:T(8,128)(2,1)S(1)} %get-tuple-element.144), channel_id=1, source_target_pairs={{0,8},{4,12},{8,0},{12,4},{16,24},{20,28},{24,16},{28,20},{32,40},... | collective-permute-start | bytes 122888 | tf_op jit(solution)/shard_map/ppermute | solution.py:796
  40.5 3.1 %collective-permute-start.10 = (bf16[80,256]{1,0:T(8,128)(2,1)S(1)}, bf16[80,256]{1,0:T(8,128)(2,1)S(1)}, u32[]{:S(2)}, u32[]{:S(2)}) collective-permute-start(bf16[80,256]{1,0:T(8,128)(2,1)S(1)} %get-tuple-element.145), channel_id=1, source_target_pairs={{0,12},{4,0},{8,4},{12,8},{16,28},{20,16},{24,20},{28,24},{32,44},... | collective-permute-start | bytes 122888 | tf_op jit(solution)/shard_map/ppermute | solution.py:796
  44.3 21.5 %collective-permute-start.13 = (bf16[80,256]{1,0:T(8,128)(2,1)S(1)}, bf16[80,256]{1,0:T(8,128)(2,1)S(1)}, u32[]{:S(2)}, u32[]{:S(2)}) collective-permute-start(bf16[80,256]{1,0:T(8,128)(2,1)S(1)} %get-tuple-element.161.own), channel_id=1, source_target_pairs={{0,48},{4,52},{8,56},{12,60},{16,0},{20,4},{24,8},{28,12},{32,16},... | collective-permute-start | bytes 122888 | tf_op jit(solution)/shard_map/ppermute | solution.py:796
  49.7 17.5 %collective-permute-start.12 = (bf16[80,256]{1,0:T(8,128)(2,1)S(1)}, bf16[80,256]{1,0:T(8,128)(2,1)S(1)}, u32[]{:S(2)}, u32[]{:S(2)}) collective-permute-start(bf16[80,256]{1,0:T(8,128)(2,1)S(1)} %get-tuple-element.161.own), channel_id=1, source_target_pairs={{0,32},{4,36},{8,40},{12,44},{16,48},{20,52},{24,56},{28,60},{32,0... | collective-permute-start | bytes 122888 | tf_op jit(solution)/shard_map/ppermute | solution.py:796
  62.2 6.3 %collective-permute-start.11 = (bf16[80,256]{1,0:T(8,128)(2,1)S(1)}, bf16[80,256]{1,0:T(8,128)(2,1)S(1)}, u32[]{:S(2)}, u32[]{:S(2)}) collective-permute-start(bf16[80,256]{1,0:T(8,128)(2,1)S(1)} %get-tuple-element.161.own), channel_id=1, source_target_pairs={{0,16},{4,20},{8,24},{12,28},{16,32},{20,36},{24,40},{28,44},{32,4... | collective-permute-start | bytes 122888 | tf_op jit(solution)/shard_map/ppermute | solution.py:796
  69.2 14.0 %copy-start.1 = (f32[256]{0:T(256)S(1)}, f32[256]{0:T(256)}, u32[]{:S(2)}) copy-start(f32[256]{0:T(256)} %param.25) | copy-start | bytes 3076
  69.2 7.3 %collective-permute-start.16 = (bf16[80,256]{1,0:T(8,128)(2,1)S(1)}, bf16[80,256]{1,0:T(8,128)(2,1)S(1)}, u32[]{:S(2)}, u32[]{:S(2)}) collective-permute-start(bf16[80,256]{1,0:T(8,128)(2,1)S(1)} %get-tuple-element.175), channel_id=1, source_target_pairs={{0,192},{4,196},{8,200},{12,204},{16,208},{20,212},{24,216},{28,22... | collective-permute-start | bytes 122888 | tf_op jit(solution)/shard_map/ppermute | solution.py:796
  71.9 5.5 %collective-permute-start.15 = (bf16[80,256]{1,0:T(8,128)(2,1)S(1)}, bf16[80,256]{1,0:T(8,128)(2,1)S(1)}, u32[]{:S(2)}, u32[]{:S(2)}) collective-permute-start(bf16[80,256]{1,0:T(8,128)(2,1)S(1)} %get-tuple-element.175), channel_id=1, source_target_pairs={{0,128},{4,132},{8,136},{12,140},{16,144},{20,148},{24,152},{28,15... | collective-permute-start | bytes 122888 | tf_op jit(solution)/shard_map/ppermute | solution.py:796
  72.5 5.3 %collective-permute-start.14 = (bf16[80,256]{1,0:T(8,128)(2,1)S(1)}, bf16[80,256]{1,0:T(8,128)(2,1)S(1)}, u32[]{:S(2)}, u32[]{:S(2)}) collective-permute-start(bf16[80,256]{1,0:T(8,128)(2,1)S(1)} %get-tuple-element.175), channel_id=1, source_target_pairs={{0,64},{4,68},{8,72},{12,76},{16,80},{20,84},{24,88},{28,92},{32,9... | collective-permute-start | bytes 122888 | tf_op jit(solution)/shard_map/ppermute | solution.py:796
  78.5 3.4 %collective-permute-start.17 = (bf16[64,256]{1,0:T(8,128)(2,1)S(1)}, bf16[64,256]{1,0:T(8,128)(2,1)S(1)}, u32[]{:S(2)}, u32[]{:S(2)}) collective-permute-start(bf16[64,256]{1,0:T(8,128)(2,1)S(1)} %get-tuple-element.205), channel_id=1, source_target_pairs={{0,4},{4,8},{8,12},{12,0},{16,20},{20,24},{24,28},{28,16},{32,36},... | collective-permute-start | bytes 98312 | tf_op jit(solution)/shard_map/ppermute | solution.py:796
  78.6 4.0 %collective-permute-start.18 = (bf16[64,256]{1,0:T(8,128)(2,1)S(1)}, bf16[64,256]{1,0:T(8,128)(2,1)S(1)}, u32[]{:S(2)}, u32[]{:S(2)}) collective-permute-start(bf16[64,256]{1,0:T(8,128)(2,1)S(1)} %get-tuple-element.206), channel_id=1, source_target_pairs={{0,8},{4,12},{8,0},{12,4},{16,24},{20,28},{24,16},{28,20},{32,40},... | collective-permute-start | bytes 98312 | tf_op jit(solution)/shard_map/ppermute | solution.py:796
  80.2 3.0 %collective-permute-start.19 = (bf16[64,256]{1,0:T(8,128)(2,1)S(1)}, bf16[64,256]{1,0:T(8,128)(2,1)S(1)}, u32[]{:S(2)}, u32[]{:S(2)}) collective-permute-start(bf16[64,256]{1,0:T(8,128)(2,1)S(1)} %get-tuple-element.207), channel_id=1, source_target_pairs={{0,12},{4,0},{8,4},{12,8},{16,28},{20,16},{24,20},{28,24},{32,44},... | collective-permute-start | bytes 98312 | tf_op jit(solution)/shard_map/ppermute | solution.py:796
  85.9 8.9 %copy-start.13 = (bf16[16,256]{1,0:T(8,128)(2,1)S(1)}, bf16[16,256]{1,0:T(8,128)(2,1)}, u32[]{:S(2)}) copy-start(bf16[16,256]{1,0:T(8,128)(2,1)} %constant.60.clone.spread) | copy-start | bytes 24580
  88.8 5.2 %collective-permute-start.22 = (f32[2,2048]{1,0:T(2,128)S(1)}, f32[2,2048]{1,0:T(2,128)S(1)}, u32[]{:S(2)}, u32[]{:S(2)}) collective-permute-start(f32[2,2048]{1,0:T(2,128)S(1)} %get-tuple-element.220.s0), channel_id=1, source_target_pairs={{0,3},{1,0},{2,1},{3,2},{4,7},{5,4},{6,5},{7,6},{8,11},{9,8},{10,9... | collective-permute-start | bytes 49160 | tf_op jit(solution)/shard_map/ppermute | solution.py:729
  88.9 5.3 %collective-permute-start.21 = (f32[2,2048]{1,0:T(2,128)S(1)}, f32[2,2048]{1,0:T(2,128)S(1)}, u32[]{:S(2)}, u32[]{:S(2)}) collective-permute-start(f32[2,2048]{1,0:T(2,128)S(1)} %get-tuple-element.220.s0), channel_id=1, source_target_pairs={{0,2},{1,3},{2,0},{3,1},{4,6},{5,7},{6,4},{7,5},{8,10},{9,11},{10,... | collective-permute-start | bytes 49160 | tf_op jit(solution)/shard_map/ppermute | solution.py:729
  90.8 4.1 %collective-permute-start.20 = (f32[2,2048]{1,0:T(2,128)S(1)}, f32[2,2048]{1,0:T(2,128)S(1)}, u32[]{:S(2)}, u32[]{:S(2)}) collective-permute-start(f32[2,2048]{1,0:T(2,128)S(1)} %get-tuple-element.220.s0), channel_id=1, source_target_pairs={{0,1},{1,2},{2,3},{3,0},{4,5},{5,6},{6,7},{7,4},{8,9},{9,10},{10,1... | collective-permute-start | bytes 49160 | tf_op jit(solution)/shard_map/ppermute | solution.py:729
  96.5 9.2 %collective-permute-start.25 = (bf16[1024,128]{1,0:T(8,128)(2,1)S(1)}, bf16[1024,128]{1,0:T(8,128)(2,1)S(1)}, u32[]{:S(2)}, u32[]{:S(2)}) collective-permute-start(bf16[1024,128]{1,0:T(8,128)(2,1)S(1)} %get-tuple-element.228), channel_id=1, source_target_pairs={{0,3},{1,0},{2,1},{3,2},{4,7},{5,4},{6,5},{7,6},{8,11},{9,8},{10,9... | collective-permute-start | bytes 786440 | tf_op jit(solution)/shard_map/ppermute | solution.py:729
  100.1 9.3 %collective-permute-start.24 = (bf16[1024,128]{1,0:T(8,128)(2,1)S(1)}, bf16[1024,128]{1,0:T(8,128)(2,1)S(1)}, u32[]{:S(2)}, u32[]{:S(2)}) collective-permute-start(bf16[1024,128]{1,0:T(8,128)(2,1)S(1)} %get-tuple-element.226), channel_id=1, source_target_pairs={{0,1},{1,2},{2,3},{3,0},{4,5},{5,6},{6,7},{7,4},{8,9},{9,10},{10,1... | collective-permute-start | bytes 786440 | tf_op jit(solution)/shard_map/ppermute | solution.py:729
  101.5 13.5 %collective-permute-start.27 = (bf16[1024,128]{1,0:T(8,128)(2,1)S(1)}, bf16[1024,128]{1,0:T(8,128)(2,1)S(1)}, u32[]{:S(2)}, u32[]{:S(2)}) collective-permute-start(bf16[1024,128]{1,0:T(8,128)(2,1)S(1)} %get-tuple-element.231), channel_id=1, source_target_pairs={{0,1},{1,2},{2,3},{3,0},{4,5},{5,6},{6,7},{7,4},{8,9},{9,10},{10,1... | collective-permute-start | bytes 786440 | tf_op jit(solution)/shard_map/ppermute | solution.py:729
  103.2 11.8 %collective-permute-start.23 = (bf16[1024,128]{1,0:T(8,128)(2,1)S(1)}, bf16[1024,128]{1,0:T(8,128)(2,1)S(1)}, u32[]{:S(2)}, u32[]{:S(2)}) collective-permute-start(bf16[1024,128]{1,0:T(8,128)(2,1)S(1)} %get-tuple-element.224), channel_id=1, source_target_pairs={{0,3},{1,0},{2,1},{3,2},{4,7},{5,4},{6,5},{7,6},{8,11},{9,8},{10,9... | collective-permute-start | bytes 786440 | tf_op jit(solution)/shard_map/ppermute | solution.py:729
  109.5 8.7 %collective-permute-start.26 = (bf16[1024,128]{1,0:T(8,128)(2,1)S(1)}, bf16[1024,128]{1,0:T(8,128)(2,1)S(1)}, u32[]{:S(2)}, u32[]{:S(2)}) collective-permute-start(bf16[1024,128]{1,0:T(8,128)(2,1)S(1)} %get-tuple-element.229), channel_id=1, source_target_pairs={{0,1},{1,2},{2,3},{3,0},{4,5},{5,6},{6,7},{7,4},{8,9},{9,10},{10,1... | collective-permute-start | bytes 786440 | tf_op jit(solution)/shard_map/ppermute | solution.py:729
  112.2 7.6 %collective-permute-start.28 = (bf16[1024,128]{1,0:T(8,128)(2,1)S(1)}, bf16[1024,128]{1,0:T(8,128)(2,1)S(1)}, u32[]{:S(2)}, u32[]{:S(2)}) collective-permute-start(bf16[1024,128]{1,0:T(8,128)(2,1)S(1)} %get-tuple-element.232), channel_id=1, source_target_pairs={{0,3},{1,0},{2,1},{3,2},{4,7},{5,4},{6,5},{7,6},{8,11},{9,8},{10,9... | collective-permute-start | bytes 786440 | tf_op jit(solution)/shard_map/ppermute | solution.py:729
  (11 other events, 38.4 us)
